TPU v7x, 128 devices: a whole 4x4x4 slice. The times are simulated.
128 devices in a mesh: seq: 8 (over z, core), tp: 16 (over y, x).
Axes of the slice: x: 4, y: 4, z: 4, core: 2. Of those that a mesh axis runs over, the one named last changes fastest.
Arguments:
- block_input: float32 [2, 8192, 1024], P(None, 'seq'), may hold values from -6 to 6
- first_gain: float32 [1024], replicated, may hold values from 0.1 to 1.9
- in_weight: bfloat16 [1024, 3, 1024], P(None, None, 'tp'), may hold values from -0.1875 to 0.1875
- conv_taps: float32 [3, 1024], P(None, 'tp'), may hold values from -2.5 to 2.5
- out_weight: bfloat16 [1024, 1024], P('tp'), may hold values from -0.1875 to 0.1875
- second_gain: float32 [1024], replicated, may hold values from 0.1 to 1.9
- gate_weight: bfloat16 [1024, 4608], P(None, 'tp'), may hold values from -0.1875 to 0.1875
- up_weight: bfloat16 [1024, 4608], P(None, 'tp'), may hold values from -0.1875 to 0.1875
- down_weight: bfloat16 [4608, 1024], P('tp'), may hold values from -0.09375 to 0.09375
- doc_starts: int32 [2, 8], replicated, may hold values from 0 to 8191, as said below
- out_cotangent: float32 [2, 8192, 1024], P(None, 'seq'), may hold values from -6 to 6
Outputs:
- block_output: float32 [2, 8192, 1024], P(None, 'seq')
- input_grad: float32 [2, 8192, 1024], P(None, 'seq')
- first_gain_grad: float32 [1024], replicated
- in_weight_grad: float32 [1024, 3, 1024], P(None, None, 'tp')
- conv_taps_grad: float32 [3, 1024], P(None, 'tp')
- out_weight_grad: float32 [1024, 1024], P('tp')
- second_gain_grad: float32 [1024], replicated
- gate_weight_grad: float32 [1024, 4608], P(None, 'tp')
- up_weight_grad: float32 [1024, 4608], P(None, 'tp')
- down_weight_grad: float32 [4608, 1024], P('tp')
Inputs may be any that keep to these rules, and one draw needn't show every extreme that they name: `doc_starts`: each row lists the first positions of the 8 documents packed into one sequence, strictly increasing, the first one 0; the last document ends at 8192.
All inputs are finite; a program needn't handle non-finite values.
Results may differ from a plain program's by a relative error of at most 0.024.
Values may be sent and summed in bfloat16 or wider, within the bound.
No kernel may reach another device: no remote copies, remote signals or barrier semaphores. Data moves between devices by JAX's collectives and lax.ppermute only.
A program may use at most 192 MiB of HBM per device.

v0:
```python
import jax
import jax.numpy as jnp
from jax import lax
from jax.sharding import PartitionSpec as P

epsilon = 1e-05


def shifted(value, axis, steps):
    count = lax.axis_size(axis)
    initial, last = (max(0, -steps), min(count, count - steps))
    return lax.ppermute(value, axis, [(source, source + steps) for source in range(initial, last)])


def doc_index(doc_starts, positions):
    hits = (doc_starts[:, None, :] <= positions[None, :, None]).astype(jnp.int32)
    return jnp.sum(hits, axis=-1) - 1


def contract_rows(left, right):
    return lax.dot_general(
        left, right, (((0,), (0,)), ((), ())), preferred_element_type=jnp.float32
    )


def contract_last(left, right):
    return lax.dot_general(
        left, right, (((1,), (1,)), ((), ())), preferred_element_type=jnp.float32
    )


def shards(
    block_input,
    first_gain,
    in_weight,
    conv_taps,
    out_weight,
    second_gain,
    gate_weight,
    up_weight,
    down_weight,
    doc_starts,
    out_cotangent,
):
    seq_count, seg_len, model_width = block_input.shape
    chan_count = in_weight.shape[2]
    row_count = seq_count * seg_len
    positions = lax.axis_index("seq") * seg_len + jnp.arange(seg_len, dtype=jnp.int32)
    current = doc_index(doc_starts, positions)
    one_back = (doc_index(doc_starts, positions - 1) == current).astype(jnp.float32)[..., None]
    two_back = (doc_index(doc_starts, positions - 2) == current).astype(jnp.float32)[..., None]
    flat_input = block_input.reshape(row_count, model_width)
    inverse_one = lax.rsqrt(jnp.mean(flat_input * flat_input, axis=-1, keepdims=True) + epsilon)
    normed1 = (flat_input * inverse_one * first_gain).astype(jnp.bfloat16)
    in_flat = in_weight.reshape(model_width, 3 * chan_count)
    projected = jnp.dot(normed1, in_flat, preferred_element_type=jnp.float32).reshape(
        seq_count, seg_len, 3, chan_count
    )
    b_gate = projected[:, :, 0]
    c_gate = projected[:, :, 1]
    x_gate = projected[:, :, 2]
    product = (b_gate * x_gate).astype(jnp.bfloat16)
    carried = shifted(product[:, seg_len - 2 :], "seq", 1)
    extended = jnp.concatenate([carried, product], axis=1).astype(jnp.float32)
    prev_one = extended[:, 1 : seg_len + 1]
    prev_two = extended[:, :seg_len]
    current_product = product.astype(jnp.float32)
    convolved = (
        conv_taps[0] * current_product
        + conv_taps[1] * one_back * prev_one
        + conv_taps[2] * two_back * prev_two
    )
    mixer_in = (c_gate * convolved).astype(jnp.bfloat16).reshape(row_count, chan_count)
    mixer_part = jnp.dot(mixer_in, out_weight, preferred_element_type=jnp.float32)
    residual = flat_input + lax.psum(mixer_part, "tp")
    inverse_two = lax.rsqrt(jnp.mean(residual * residual, axis=-1, keepdims=True) + epsilon)
    normed_rows = (residual * inverse_two * second_gain).astype(jnp.bfloat16)
    gate_proj = jnp.dot(normed_rows, gate_weight, preferred_element_type=jnp.float32)
    up_proj = jnp.dot(normed_rows, up_weight, preferred_element_type=jnp.float32)
    sigmoid_gate = jax.nn.sigmoid(gate_proj)
    activated = gate_proj * sigmoid_gate
    hidden = (activated * up_proj).astype(jnp.bfloat16)
    ffn_part = jnp.dot(hidden, down_weight, preferred_element_type=jnp.float32)
    block_output = residual + lax.psum(ffn_part.astype(jnp.bfloat16), "tp").astype(jnp.float32)
    block_output = block_output.reshape(seq_count, seg_len, model_width)
    grad_out = out_cotangent.reshape(row_count, model_width)
    grad_low = grad_out.astype(jnp.bfloat16)
    down_grad = contract_rows(hidden, grad_low)
    d_hidden = contract_last(grad_low, down_weight)
    d_gate = (d_hidden * up_proj * sigmoid_gate * (1.0 + gate_proj * (1.0 - sigmoid_gate))).astype(
        jnp.bfloat16
    )
    d_up = (d_hidden * activated).astype(jnp.bfloat16)
    gate_grad = contract_rows(normed_rows, d_gate)
    up_grad = contract_rows(normed_rows, d_up)
    d_normed2_part = contract_last(d_gate, gate_weight) + contract_last(d_up, up_weight)
    d_normed2 = lax.psum(d_normed2_part.astype(jnp.bfloat16), "tp").astype(jnp.float32)
    scaled_two = second_gain * d_normed2
    second_grad = jnp.sum(d_normed2 * residual * inverse_two, axis=0)
    d_residual = grad_out + inverse_two * (
        scaled_two
        - residual
        * inverse_two
        * inverse_two
        * jnp.mean(scaled_two * residual, axis=-1, keepdims=True)
    )
    d_low_rows = d_residual.astype(jnp.bfloat16)
    out_grad = contract_rows(mixer_in, d_low_rows)
    d_mixer = contract_last(d_low_rows, out_weight).reshape(seq_count, seg_len, chan_count)
    d_conv = d_mixer * c_gate
    d_cgate = d_mixer * convolved
    lag_one = one_back * d_conv
    lag_two = two_back * d_conv
    next_one, next_two = shifted((lag_one[:, :2], lag_two[:, :2]), "seq", -1)
    ahead_one = jnp.concatenate([lag_one, next_one], axis=1)[:, 1 : seg_len + 1]
    ahead_two = jnp.concatenate([lag_two, next_two], axis=1)[:, 2 : seg_len + 2]
    d_product = conv_taps[0] * d_conv + conv_taps[1] * ahead_one + conv_taps[2] * ahead_two
    taps_grad = jnp.stack(
        [
            jnp.sum(d_conv * current_product, axis=(0, 1)),
            jnp.sum(lag_one * prev_one, axis=(0, 1)),
            jnp.sum(lag_two * prev_two, axis=(0, 1)),
        ]
    )
    d_projected = (
        jnp.stack([d_product * x_gate, d_cgate, d_product * b_gate], axis=2)
        .astype(jnp.bfloat16)
        .reshape(row_count, 3 * chan_count)
    )
    in_grad = contract_rows(normed1, d_projected).reshape(model_width, 3, chan_count)
    d_normed1_part = contract_last(d_projected, in_flat)
    d_normed1 = lax.psum(d_normed1_part.astype(jnp.bfloat16), "tp").astype(jnp.float32)
    scaled_one = first_gain * d_normed1
    first_grad = jnp.sum(d_normed1 * flat_input * inverse_one, axis=0)
    input_grad = d_residual + inverse_one * (
        scaled_one
        - flat_input
        * inverse_one
        * inverse_one
        * jnp.mean(scaled_one * flat_input, axis=-1, keepdims=True)
    )
    input_grad = input_grad.reshape(seq_count, seg_len, model_width)
    first_grad, in_grad, taps_grad, out_grad, second_grad, gate_grad, up_grad, down_grad = (
        lax.psum(first_grad.astype(jnp.bfloat16), "seq").astype(jnp.float32),
        lax.psum(in_grad.astype(jnp.bfloat16), "seq").astype(jnp.float32),
        lax.psum(taps_grad.astype(jnp.bfloat16), "seq").astype(jnp.float32),
        lax.psum(out_grad.astype(jnp.bfloat16), "seq").astype(jnp.float32),
        lax.psum(second_grad.astype(jnp.bfloat16), "seq").astype(jnp.float32),
        lax.psum(gate_grad.astype(jnp.bfloat16), "seq").astype(jnp.float32),
        lax.psum(up_grad.astype(jnp.bfloat16), "seq").astype(jnp.float32),
        lax.psum(down_grad.astype(jnp.bfloat16), "seq").astype(jnp.float32),
    )
    return (
        block_output,
        input_grad,
        first_grad,
        in_grad,
        taps_grad,
        out_grad,
        second_grad,
        gate_grad,
        up_grad,
        down_grad,
    )


def solution(mesh):
    return jax.shard_map(
        shards,
        mesh=mesh,
        in_specs=(
            P(None, "seq", None),
            P(),
            P(None, None, "tp"),
            P(None, "tp"),
            P("tp", None),
            P(),
            P(None, "tp"),
            P(None, "tp"),
            P("tp", None),
            P(),
            P(None, "seq", None),
        ),
        out_specs=(
            P(None, "seq", None),
            P(None, "seq", None),
            P(),
            P(None, None, "tp"),
            P(None, "tp"),
            P("tp", None),
            P(),
            P(None, "tp"),
            P(None, "tp"),
            P("tp", None),
        ),
        check_vma=False,
    )
```

profile of v0, /device:TPU:65, one launch (start us, length us, event | category | flops | bytes accessed | tf_op | source)
XLA Modules:
  0.0 586.4 jit_solution(7673690265563639940)
XLA Ops:
  7.3 4.2 multiply_reduce_fusion.1
  11.4 0.6 fusion.40
  12.0 1.0 copy-done.1
  13.0 0.9 multiply_convert_fusion.1
  14.0 1.5 fusion.16
  15.7 0.4 copy-done.5
  16.1 3.8 collective-permute-start
  20.2 0.7 collective-permute-done
  20.9 0.1 maximum_convert_fusion.1
  21.1 0.3 fusion.37
  21.4 4.7 fusion.42
  26.1 0.2 all-reduce.10.cloned.1.call-start
  26.4 6.1 %bitcast_convert_fusion = bf16[2048,1024]{1,0:T(8,128)(2,1)} fusion(f32[2,1024,1024]{2,1,0:T(8,128)} %param.21), kind=kLoop, calls=%fused_computation.18 | loop fusion | flops 2097152 | bytes 12582912 | tf_op jit(solution)/shard_map/convert_element_type | solution.py:87
  32.4 136.8 %all-reduce.8.cloned.1.call-done = f32[2048,1024]{1,0:T(8,128)} async-done(((f32[2048,1024]{1,0:T(8,128)}), f32[2048,1024]{1,0:T(8,128)}) %all-reduce.8.cloned.1.call-update) | async-done | bytes 8388624 | tf_op jit(solution)/shard_map/psum | solution.py:75
  169.2 10.1 %multiply_reduce_fusion = (f32[2048]{0:T(1024)S(1)}, f32[2048,1024]{1,0:T(8,128)}) fusion(f32[2048,1024]{1,0:T(8,128)} %all-reduce.8.cloned.1.call-done, f32[2,1024,1024]{2,1,0:T(8,128)} %param.11), kind=kLoop, calls=%fused_computation.26 | loop fusion | flops 6289408 | bytes 25174016 | tf_op jit(solution)/shard_map/reduce_sum | solution.py:76
  179.3 4.0 multiply_convert_fusion
  183.3 1.4 fusion.44
  184.8 0.5 copy-done.9
  185.2 1.4 fusion.43
  186.7 0.7 copy-done.7
  187.4 3.3 multiply_convert_fusion.2
  190.7 2.4 fusion.45
  193.1 4.6 add_convert_fusion
  197.7 0.3 all-reduce.14.cloned.1.call-start
  198.2 0.4 copy.34
  198.6 0.2 copy.42
  198.7 0.4 copy.35
  199.2 1.0 copy.43
  200.2 0.5 copy-done.15
  200.7 2.2 convolution_convert_fusion.2
  203.0 2.2 convolution_convert_fusion.3
  205.2 0.5 copy-done.40
  205.7 2.2 convolution_convert_fusion.4
  207.9 92.5 %all-reduce.10.cloned.1.call-done = bf16[2048,1024]{1,0:T(8,128)(2,1)} async-done(((bf16[2048,1024]{1,0:T(8,128)(2,1)}), bf16[2048,1024]{1,0:T(8,128)(2,1)}) %all-reduce.10.cloned.1.call-update) | async-done | bytes 4194320 | tf_op jit(solution)/shard_map/psum | solution.py:97
  300.5 6.7 %fusion.11 = (bf16[1024]{0:T(1024)(128)(2,1)}, f32[2048]{0:T(1024)S(1)}) fusion(f32[2048,1024]{1,0:T(8,128)} %get-tuple-element.34, bf16[2048,1024]{1,0:T(8,128)(2,1)} %all-reduce.10.cloned.1.call-done, f32[2048]{0:T(1024)} %copy-done.23, f32[1024]{0:T(1024)} %param.16), kind=kLoop, calls=%fused_computation.15 | loop fusion | flops 14676992 | bytes 12605440 | tf_op jit(solution)/shard_map/reduce_sum | solution.py:99
  307.2 7.1 %fusion.9 = f32[2048,1024]{1,0:T(8,128)S(1)} fusion(bf16[2048,1024]{1,0:T(8,128)(2,1)S(1)} %copy-done.4, f32[2,1024,1024]{2,1,0:T(8,128)} %param.21, f32[2048,1024]{1,0:T(8,128)} %get-tuple-element.34, f32[2048]{0:T(1024)S(1)} %broadcast_multiply_fusion.3, f32[1024]{0:T(1024)S(1)} %copy-done.26, f32[2048]{0:T(1024)S(1)} %copy-done.24), kind=kLoop, calls=%fused_computation.13 | loop fusion | flops 16777216 | bytes 29380608 | tf_op jit(solution)/shard_map/add | solution.py:100
  314.3 2.5 multiply_reduce_fusion.4
  316.8 0.4 multiply_reduce_fusion.3
  317.2 2.8 collective-permute-start.2
  320.0 2.2 collective-permute-start.1
  322.2 1.5 fusion.23
  323.7 1.9 collective-permute-done.1
  325.6 0.7 fusion.33
  326.5 0.8 copy.33
  327.3 0.2 copy.41
  327.5 1.0 copy-done.6
  328.5 1.8 convolution_convert_fusion.5
  330.3 4.4 convolution_convert_fusion.1
  334.7 3.2 convolution_convert_fusion
  338.0 0.7 copy-done.29
  338.7 54.8 %all-reduce.14.cloned.1.call-done = (bf16[1024,3,64]{0,2,1:T(8,128)(2,1)}, bf16[64,1024]{1,0:T(8,128)(2,1)}, bf16[1024,288]{0,1:T(8,128)(2,1)}, bf16[1024,288]{0,1:T(8,128)(2,1)}, bf16[288,1024]{1,0:T(8,128)(2,1)}) async-done(((bf16[1024,3,64]{0,2,1:T(8,128)(2,1)}, bf16[64,1024]{1,0:T(8,128)(2,1)}, bf16[1024,288]{0,1:T(8,128)(2,1)}, bf16[1024,288]{0,1:T(8,128)(2,1)}, bf16[288,1024]{1,0:T(8,128)(2,1)}), ...) | async-done | bytes 2293776 | tf_op jit(solution)/shard_map/psum | solution.py:145
  393.5 1.7 convert_element_type.182
  395.2 2.0 convert_element_type.176
  397.1 2.2 convert_element_type.186
  399.3 2.2 convert_element_type.188
  401.6 1.1 convert_element_type.190
  402.7 139.4 %all-reduce.12.cloned.1.call-done = (bf16[2048,1024]{1,0:T(8,128)(2,1)}, bf16[2048,1024]{1,0:T(8,128)(2,1)}) async-done(((bf16[2048,1024]{1,0:T(8,128)(2,1)}, bf16[2048,1024]{1,0:T(8,128)(2,1)}), (bf16[2048,1024]{1,0:T(8,128)(2,1)}, bf16[2048,1024]{1,0:T(8,128)(2,1)})) %all-reduce.12.cloned.1.call-update) | async-done | bytes 8388624 | tf_op jit(solution)/shard_map/psum | solution.py:84
  542.1 10.3 %convert_add_fusion = f32[2048,1024]{1,0:T(8,128)} fusion(f32[2048,1024]{1,0:T(8,128)} %get-tuple-element.34, bf16[2048,1024]{1,0:T(8,128)(2,1)} %get-tuple-element.19), kind=kLoop, calls=%fused_computation.24 | loop fusion | flops 4194304 | bytes 20971520 | tf_op jit(solution)/shard_map/add | solution.py:84
  552.5 3.2 fusion.13
  555.7 10.7 %all-reduce.1 = (bf16[1024]{0:T(1024)(128)(2,1)S(1)}, bf16[3,64]{1,0:T(4,128)(2,1)S(1)}, bf16[1024]{0:T(1024)(128)(2,1)S(1)}) all-reduce(bf16[1024]{0:T(1024)(128)(2,1)S(1)} %get-tuple-element.12, bf16[3,64]{1,0:T(4,128)(2,1)S(1)} %pad_maximum_fusion.2, bf16[1024]{0:T(1024)(128)(2,1)S(1)} %copy-done.30), channel_id=1, replica_groups=mesh['seq'=8,'tp'=16] {'seq'}, use_global_device_ids=true, to_apply=%region_12.0 | all-reduce | flops 2240 | bytes 8960 | tf_op jit(solution)/shard_map/psum | solution.py:144
  566.4 0.6 convert_element_type.173
  567.0 0.6 convert_element_type.180
  567.6 0.6 convert_element_type.184
  568.2 11.7 %fusion.6 = f32[2048,1024]{1,0:T(8,128)} fusion(f32[2048,1024]{1,0:T(8,128)} %copy-done.2, bf16[2048,1024]{1,0:T(8,128)(2,1)} %get-tuple-element.20, f32[2,1024,1024]{2,1,0:T(8,128)} %param.11, f32[2048]{0:T(1024)S(1)} %broadcast_multiply_fusion.2, f32[1024]{0:T(1024)S(1)} %copy-done.28, f32[2048]{0:T(1024)S(1)} %bitcast.180), kind=kLoop, calls=%fused_computation.10 | loop fusion | flops 16777216 | bytes 29380608 | tf_op jit(solution)/shard_map/add | solution.py:135
  (106 shorter events, 1.2 us)
Async XLA Ops:
  7.2 179.5 %copy-start = (bf16[288,1024]{1,0:T(8,128)(2,1)S(1)}, bf16[288,1024]{1,0:T(8,128)(2,1)}, u32[]{:S(2)}) copy-start(bf16[288,1024]{1,0:T(8,128)(2,1)} %param.19) | copy-start | bytes 1769476
  7.2 4.8 copy-start.27
  7.2 162.0 %all-reduce.8.cloned.1.call-start = ((), (), s32[]{:S(2)}) async-start(), calls=%async_computation | async-start | bytes 16777216 | tf_op jit(solution)/shard_map/psum | solution.py:75
  7.2 5.8 copy-start.1
  13.0 1.0 copy-start.21
  14.0 2.0 copy-start.5
  14.0 5.9 %copy-start.39 = (s32[2,8]{1,0:T(2,128)S(1)}, s32[2,8]{1,0:T(2,128)}, u32[]{:S(2)}) copy-start(s32[2,8]{1,0:T(2,128)} %param.20) | copy-start | bytes 196
  14.0 6.1 %copy-start.38 = (f32[3,64]{1,0:T(4,128)S(1)}, f32[3,64]{1,0:T(4,128)}, u32[]{:S(2)}) copy-start(f32[3,64]{1,0:T(4,128)} %param.14) | copy-start | bytes 2308
  15.6 5.9 copy-start.19
  16.1 4.8 collective-permute-start
  20.2 6.0 %copy-start.31 = (f32[64]{0:T(128)}, f32[64]{0:T(128)S(1)}, u32[]{:S(2)}) copy-start(f32[64]{0:T(128)S(1)} %get-tuple-element.45) | copy-start | bytes 772
  20.2 6.0 %copy-start.33 = (f32[64]{0:T(128)}, f32[64]{0:T(128)S(1)}, u32[]{:S(2)}) copy-start(f32[64]{0:T(128)S(1)} %get-tuple-element.46) | copy-start | bytes 772
  20.2 5.9 %copy-start.35 = (f32[64]{0:T(128)}, f32[64]{0:T(128)S(1)}, u32[]{:S(2)}) copy-start(f32[64]{0:T(128)S(1)} %get-tuple-element.47) | copy-start | bytes 772
  26.1 274.3 %all-reduce.10.cloned.1.call-start = ((), (), s32[]{:S(2)}) async-start(), calls=%async_computation.1 | async-start | bytes 8388608 | tf_op jit(solution)/shard_map/psum | solution.py:97
  32.4 146.8 %copy-start.25 = (f32[1024]{0:T(1024)S(1)}, f32[1024]{0:T(1024)}, u32[]{:S(2)}) copy-start(f32[1024]{0:T(1024)} %param.16) | copy-start | bytes 12292
  179.3 4.0 copy-start.23
  179.3 4.0 copy-start.16
  183.3 1.9 copy-start.9
  183.3 1.9 copy-start.17
  185.2 2.2 copy-start.7
  190.7 2.4 copy-start.12
  190.7 2.4 copy-start.14
  197.7 195.8 %all-reduce.14.cloned.1.call-start = ((), (), s32[]{:S(2)}) async-start(), calls=%async_computation.3 | async-start | bytes 4587520 | tf_op jit(solution)/shard_map/psum | solution.py:145
  198.0 2.2 copy-start.10
  198.0 2.7 copy-start.15
  200.7 2.2 copy-start.13
  203.0 2.2 copy-start.8
  203.0 2.7 copy-start.40
  300.5 6.7 %copy-start.4 = (bf16[2048,1024]{1,0:T(8,128)(2,1)S(1)}, bf16[2048,1024]{1,0:T(8,128)(2,1)}, u32[]{:S(2)}) copy-start(bf16[2048,1024]{1,0:T(8,128)(2,1)} %all-reduce.10.cloned.1.call-done) | copy-start | bytes 12582916
  300.5 6.7 %copy-start.24 = (f32[2048]{0:T(1024)S(1)}, f32[2048]{0:T(1024)}, u32[]{:S(2)}) copy-start(f32[2048]{0:T(1024)} %copy-done.23) | copy-start | bytes 24580
  300.5 6.7 %copy-start.26 = (f32[1024]{0:T(1024)S(1)}, f32[1024]{0:T(1024)}, u32[]{:S(2)}) copy-start(f32[1024]{0:T(1024)} %param.16) | copy-start | bytes 12292
  307.2 7.1 %copy-start.11 = (f32[8,8,2,1024]{3,1,2,0:T(8,128)S(1)}, f32[8,8,2,1024]{3,1,2,0:T(8,128)}, u32[]{:S(2)}) copy-start(f32[8,8,2,1024]{3,1,2,0:T(8,128)} %copy.43) | copy-start | bytes 1572868
  307.2 7.1 %copy-start.20 = (bf16[64,1024]{1,0:T(8,128)(2,1)S(1)}, bf16[64,1024]{1,0:T(8,128)(2,1)}, u32[]{:S(2)}) copy-start(bf16[64,1024]{1,0:T(8,128)(2,1)} %param.15) | copy-start | bytes 393220
  314.3 7.9 %copy-start.2 = (f32[2048,1024]{1,0:T(8,128)}, f32[2048,1024]{1,0:T(8,128)S(1)}, u32[]{:S(2)}) copy-start(f32[2048,1024]{1,0:T(8,128)S(1)} %fusion.9) | copy-start | bytes 25165828
  317.2 8.4 %copy-start.32 = (f32[64]{0:T(128)S(1)}, f32[64]{0:T(128)}, u32[]{:S(2)}) copy-start(f32[64]{0:T(128)} %copy-done.31) | copy-start | bytes 772
  317.2 8.4 %copy-start.34 = (f32[64]{0:T(128)S(1)}, f32[64]{0:T(128)}, u32[]{:S(2)}) copy-start(f32[64]{0:T(128)} %copy-done.33) | copy-start | bytes 772
  317.2 8.4 %copy-start.36 = (f32[64]{0:T(128)S(1)}, f32[64]{0:T(128)}, u32[]{:S(2)}) copy-start(f32[64]{0:T(128)} %copy-done.35) | copy-start | bytes 772
  317.2 6.5 %collective-permute-start.2 = (f32[2,2,64]{1,2,0:T(8,128)S(1)}, f32[2,2,64]{1,2,0:T(8,128)S(1)}, u32[]{:S(2)}, u32[]{:S(2)}) collective-permute-start(f32[2,2,64]{1,2,0:T(8,128)S(1)} %slice.62), channel_id=1, source_target_pairs={{16,0},{32,16},{48,32},{64,48},{80,64},{96,80},{112,96},{17,1},{33... | collective-permute-start | bytes 3080 | tf_op jit(solution)/shard_map/ppermute | solution.py:12
  320.0 5.6 collective-permute-start.1
  326.3 2.2 copy-start.6
  328.5 1.9 copy-start.41
  330.3 4.5 copy-start.22
  330.3 211.8 %all-reduce.12.cloned.1.call-start = ((), (), s32[]{:S(2)}) async-start(), calls=%async_computation.2 | async-start | bytes 16777216 | tf_op jit(solution)/shard_map/psum | solution.py:84
  338.0 0.7 copy-start.29
  338.0 0.7 copy-start.37
  393.5 8.1 %copy-start.18 = (bf16[288,1024]{1,0:T(8,128)(2,1)S(1)}, bf16[288,1024]{1,0:T(8,128)(2,1)}, u32[]{:S(2)}) copy-start(bf16[288,1024]{1,0:T(8,128)(2,1)} %get-tuple-element.28) | copy-start | bytes 1769476
  542.1 10.3 %slice-start = ((s8[8388608]{0:T(1024)(128)(4,1)}), s8[4194304]{0:T(1024)(128)(4,1)S(1)}, s32[]{:S(2)}) async-start(s8[8388608]{0:T(1024)(128)(4,1)} %bitcast.162), calls=%async_computation.4 | async-start | bytes 8388608
  542.1 10.3 %slice-start.1 = ((s8[8388608]{0:T(1024)(128)(4,1)}), s8[4194304]{0:T(1024)(128)(4,1)S(1)}, s32[]{:S(2)}) async-start(s8[8388608]{0:T(1024)(128)(4,1)} %bitcast.162), calls=%async_computation.5 | async-start | bytes 8388608
  542.1 10.3 %copy-start.3 = (bf16[2048,1024]{1,0:T(8,128)(2,1)S(1)}, bf16[2048,1024]{1,0:T(8,128)(2,1)}, u32[]{:S(2)}) copy-start(bf16[2048,1024]{1,0:T(8,128)(2,1)} %get-tuple-element.20) | copy-start | bytes 12582916
  542.1 10.3 %copy-start.28 = (f32[1024]{0:T(1024)S(1)}, f32[1024]{0:T(1024)}, u32[]{:S(2)}) copy-start(f32[1024]{0:T(1024)} %param.12) | copy-start | bytes 12292
  552.5 3.2 copy-start.30
Sparse Core Ops, SparseCore 0:
  26.3 142.8 all-reduce.7
  197.9 102.5 all-reduce.9
  330.4 63.0 all-reduce.13
  398.2 143.8 all-reduce.11
where the time goes:
time: 592 us; the launch traced here: 586 us
  waiting for transfers between devices  426 us (72%)
  other arithmetic  77.7 us (13%)
  matrix products  39.4 us (7%)
  between operations  14.3 us (2%)
  blocking collectives  10.7 us (2%)
  starting transfers between devices  9.32 us (2%)
  local copies, waits for them, and re-layouts  8.78 us (1%)
    psum x1, waiting for transfers between devices, shards(): lax.psum(ffn_part.astype(jnp.bfloat16), 'tp').astype(jnp.float32)  139 us
    psum x1, waiting for transfers between devices, shards(): residual = flat_input + lax.psum(mixer_part, 'tp')  137 us
    psum x1, waiting for transfers between devices, shards(): lax.psum(d_normed2_part.astype(jnp.bfloat16), 'tp').astype(jnp.float32)  92.5 us
    psum x1, waiting for transfers between devices, shards(): lax.psum(in_grad.astype(jnp.bfloat16), 'seq').astype(jnp.float32)  54.8 us
    dot_general x5, matrix products, contract_last(): lax.dot_general(left, right, (((1,), (1,)), ((), ())), preferred_element_...  16 us
  transfers between devices with their start and end apart: 7, of which 6 were waited for; matrix products, arithmetic and copies ran while one was open for 6% of the time, Pallas kernels for 0%

commit v1 on v0

v1 whole, which is shorter than its diff:
```python
import jax
import jax.numpy as jnp
from jax import lax
from jax.experimental import pallas as pl
from jax.experimental.pallas import tpu as pltpu
from jax.sharding import Mesh
from jax.sharding import PartitionSpec as P

epsilon = 1e-05
SEQ = ("z", "core")
TP = ("y", "x")
ALL = SEQ + TP
RING = 4
TPS = RING * RING
f32 = jnp.float32
bf16 = jnp.bfloat16


def turn(value, axis, steps):
    return lax.ppermute(value, axis, [(i, (i + steps) % RING) for i in range(RING)])


def ring_gather(value, axis):
    return [value, turn(value, axis, 3), turn(value, axis, 2), turn(value, axis, 1)]


def ring_gather_relay(value, axis):
    half = value.shape[0] // 2
    behind, ahead = turn(value, axis, 1), turn(value, axis, 3)
    top, bottom = turn(behind[:half], axis, 1), turn(ahead[half:], axis, 3)
    return [value, ahead, jnp.concatenate([top, bottom], axis=0), behind]


def ring_scatter(blocks, axis):
    received = [turn(blocks[k], axis, k) for k in (1, 2, 3)]
    total = blocks[0].astype(f32)
    for block in received:
        total = total + block.astype(f32)
    return total


def ring_scatter_relay(blocks, axis):
    half = blocks[2].shape[0] // 2
    low = turn(blocks[2][:half], axis, 1).astype(f32)
    high = turn(blocks[2][half:], axis, 3).astype(f32)
    first, third = blocks[1], blocks[3]
    first = jnp.concatenate([(first[:half].astype(f32) + low).astype(bf16), first[half:]], axis=0)
    third = jnp.concatenate([third[:half], (third[half:].astype(f32) + high).astype(bf16)], axis=0)
    return blocks[0].astype(f32) + turn(first, axis, 1).astype(f32) + turn(third, axis, 3).astype(f32)


def ring_total(value, axis):
    a, b, c, d = (part.astype(f32) for part in ring_gather(value, axis))
    return (a + c) + (b + d)


def plane_gather(value):
    half = value.shape[0] // 2
    top, bottom = value[:half], value[half:]
    top_x = jnp.concatenate(ring_gather(top, "x"), axis=0)
    bottom_y = jnp.concatenate(ring_gather(bottom, "y"), axis=0)
    return ring_gather_relay(top_x, "y"), ring_gather_relay(bottom_y, "x")


def plane_scatter(chunks_a, chunks_b):
    top_x = ring_scatter_relay(chunks_a, "y").astype(bf16)
    bottom_y = ring_scatter_relay(chunks_b, "x").astype(bf16)
    rows = top_x.shape[0] // RING
    top = ring_scatter([top_x[rows * k : rows * (k + 1)] for k in range(RING)], "x")
    bottom = ring_scatter([bottom_y[rows * k : rows * (k + 1)] for k in range(RING)], "y")
    return jnp.concatenate([top, bottom], axis=0)


def plane_exchange(blocks):
    moved = [blocks[:, 0]] + [None] * 3
    for k in (1, 2, 3):
        moved[RING - k] = turn(blocks[:, k], "x", k)
    moved = jnp.stack(moved, axis=1)
    out = [moved[0]] + [None] * 3
    for k in (1, 2, 3):
        out[RING - k] = turn(moved[k], "y", k)
    return jnp.stack(out, axis=0)


def rolled(value, axis, start):
    twice = jnp.concatenate([value, value], axis=axis)
    return lax.dynamic_slice_in_dim(twice, start, RING, axis=axis)


def to_relative(value):
    y, x = lax.axis_index("y"), lax.axis_index("x")
    return rolled(rolled(value, 0, y), 1, x)


def to_absolute(value):
    y, x = lax.axis_index("y"), lax.axis_index("x")
    return rolled(rolled(value, 0, (RING - y) % RING), 1, (RING - x) % RING)


def plane_tables():
    y, x = lax.axis_index("y"), lax.axis_index("x")
    i = jnp.arange(TPS, dtype=jnp.int32)
    first, second = i // RING, i % RING
    from_a = ((first + y) % RING) * RING + (second + x) % RING
    from_b = ((second + y) % RING) * RING + (first + x) % RING
    a, b = (first - y) % RING, (second - x) % RING
    return from_a, from_b, a * RING + b, b * RING + a


def relative_rows(rows, from_a, from_b):
    half, width = rows.shape[0] // TPS // 2, rows.shape[1]
    view = rows.reshape(2 * TPS, half, width)

    def body(ia, ib, top, bottom, out_a, out_b):
        out_a[...] = top[...].astype(bf16)
        out_b[...] = bottom[...].astype(bf16)

    block = (1, half, width)
    return pl.pallas_call(
        body,
        grid_spec=pltpu.PrefetchScalarGridSpec(
            num_scalar_prefetch=2,
            grid=(TPS,),
            in_specs=[
                pl.BlockSpec(block, lambda i, ia, ib: (2 * ia[i], 0, 0)),
                pl.BlockSpec(block, lambda i, ia, ib: (2 * ib[i] + 1, 0, 0)),
            ],
            out_specs=[pl.BlockSpec(block, lambda i, ia, ib: (i, 0, 0))] * 2,
        ),
        out_shape=[jax.ShapeDtypeStruct((TPS, half, width), bf16)] * 2,
        name="relative_rows",
    )(from_a, from_b, view, view)


def absolute_rows(part_a, part_b, to_a, to_b):
    _, half, width = part_a.shape

    def body(ia, ib, top, bottom, out):
        out[0, :half] = top[0].astype(f32)
        out[0, half:] = bottom[0].astype(f32)

    block = (1, half, width)
    out = pl.pallas_call(
        body,
        grid_spec=pltpu.PrefetchScalarGridSpec(
            num_scalar_prefetch=2,
            grid=(TPS,),
            in_specs=[
                pl.BlockSpec(block, lambda i, ia, ib: (ia[i], 0, 0)),
                pl.BlockSpec(block, lambda i, ia, ib: (ib[i], 0, 0)),
            ],
            out_specs=pl.BlockSpec((1, 2 * half, width), lambda i, ia, ib: (i, 0, 0)),
        ),
        out_shape=jax.ShapeDtypeStruct((TPS, 2 * half, width), f32),
        name="absolute_rows",
    )(to_a, to_b, part_a, part_b)
    return out.reshape(TPS * 2 * half, width)


def dot(left, right, left_dim, right_dim, kind=f32):
    out = lax.dot_general(
        left, right, (((left_dim,), (right_dim,)), ((), ())), preferred_element_type=f32
    )
    return out.astype(kind)


def doc_index(doc_starts, positions):
    hits = (doc_starts[:, None, :] <= positions[None, :, None]).astype(jnp.int32)
    return jnp.sum(hits, axis=-1) - 1


def shards(
    block_input,
    first_gain,
    in_weight,
    conv_taps,
    out_weight,
    second_gain,
    gate_weight,
    up_weight,
    down_weight,
    doc_starts,
    out_cotangent,
):
    seqs, seg, width = block_input.shape
    chans = in_weight.shape[2]
    ff = gate_weight.shape[1]
    count = seqs * seg
    own = count // TPS
    per_seq = TPS // seqs
    y, x = lax.axis_index("y"), lax.axis_index("x")
    place = y * RING + x
    seq = lax.axis_index(SEQ)
    from_a, from_b, to_a, to_b = plane_tables()

    positions = seq * seg + jnp.arange(seg, dtype=jnp.int32)
    current = doc_index(doc_starts, positions)
    one_back = (doc_index(doc_starts, positions - 1) == current).astype(f32)
    two_back = (doc_index(doc_starts, positions - 2) == current).astype(f32)

    out_a, out_b = plane_gather(out_weight)
    out_rel_a = jnp.concatenate(out_a, axis=0)
    out_rel_b = jnp.concatenate(out_b, axis=0)
    in_wt = jnp.transpose(in_weight, (1, 2, 0))
    share = chans // 8
    in_share = lax.dynamic_slice_in_dim(in_wt, seq * share, share, axis=1)
    in_all = lax.all_gather(in_share, ALL, axis=0, tiled=False)
    in_all = in_all.reshape(8, TPS, 3, share, width).transpose(2, 1, 0, 3, 4)
    in_all = in_all.reshape(3 * TPS * chans, width)
    taps = jnp.stack(ring_gather(conv_taps, "x"), axis=0)
    taps = jnp.stack(ring_gather(taps, "y"), axis=0)
    taps = to_absolute(taps).reshape(TPS, 3, chans).transpose(1, 0, 2).reshape(3, TPS * chans)

    flat_input = block_input.reshape(count, width)
    inverse_one = lax.rsqrt(jnp.mean(flat_input * flat_input, axis=-1, keepdims=True) + epsilon)
    normed1 = (flat_input * inverse_one * first_gain).astype(bf16)
    last = normed1.reshape(seqs, seg, width)[:, seg - 8 :]
    carried = lax.ppermute(
        last, ALL, [(i, i + TPS) for i in range(7 * TPS)]
    )
    in_flat = in_wt.reshape(3 * chans, width)
    mixer_blocks = []
    for s in range(seqs):
        proj = dot(in_flat, normed1[s * seg : (s + 1) * seg], 1, 1)
        edge = dot(in_flat, carried[s], 1, 1)
        product = (proj[:chans] * proj[2 * chans :]).astype(bf16)
        before = (edge[:chans] * edge[2 * chans :]).astype(bf16)
        extended = jnp.concatenate([before[:, 6:], product], axis=1).astype(f32)
        convolved = (
            conv_taps[0][:, None] * product.astype(f32)
            + conv_taps[1][:, None] * one_back[s] * extended[:, 1 : seg + 1]
            + conv_taps[2][:, None] * two_back[s] * extended[:, :seg]
        )
        mixed = (proj[chans : 2 * chans] * convolved).astype(bf16)
        mixer_blocks.append(mixed.reshape(chans, per_seq, own).transpose(1, 0, 2))
    mixer_blocks = jnp.concatenate(mixer_blocks, axis=0).reshape(RING, RING, chans, own)
    mixer = plane_exchange(to_relative(mixer_blocks))
    half = chans // 2
    mixer_a = mixer[:, :, :half].reshape(TPS * half, own)
    mixer_b = mixer[:, :, half:].transpose(1, 0, 2, 3).reshape(TPS * half, own)

    rows_in = lax.dynamic_slice_in_dim(flat_input, place * own, own, axis=0)
    residual = rows_in + (dot(mixer_a, out_rel_a, 0, 0) + dot(mixer_b, out_rel_b, 0, 0))
    inverse_two = lax.rsqrt(jnp.mean(residual * residual, axis=-1, keepdims=True) + epsilon)
    normed2 = (residual * inverse_two * second_gain).astype(bf16)

    norm_a, norm_b = plane_gather(normed2)
    grad_a, grad_b = relative_rows(out_cotangent.reshape(count, width), from_a, from_b)
    grad_low = [g.reshape(RING, count // 8, width) for g in (grad_a, grad_b)]
    gate_t, up_t = gate_weight.T, up_weight.T
    both_t = jnp.concatenate([gate_t, up_t], axis=0)
    chunks, halves, hiddens, downs, ups = norm_a + norm_b, [], [], [], []
    for index, chunk in enumerate(chunks):
        low = grad_low[index // RING][index % RING]
        d_hidden = dot(low, down_weight, 1, 1)
        both = dot(chunk, both_t, 1, 1)
        gate, up = both[:, :ff], both[:, ff:]
        sig = jax.nn.sigmoid(gate)
        act = gate * sig
        hidden = (act * up).astype(bf16)
        d_gate = (d_hidden * up * sig * (1.0 + gate * (1.0 - sig))).astype(bf16)
        d_up = (d_hidden * act).astype(bf16)
        d_both = jnp.concatenate([d_gate, d_up], axis=1)
        hiddens.append(hidden)
        halves.append(d_both)
        ups.append(dot(d_both, both_t, 1, 0, bf16))
        downs.append(dot(hidden, down_weight, 1, 0, bf16))
    d_normed2 = plane_scatter(ups[:RING], ups[RING:])
    ffn = plane_scatter(downs[:RING], downs[RING:])
    all_low = jnp.concatenate([g.reshape(count // 2, width) for g in grad_low], axis=0)
    ffn_grads = jnp.concatenate(
        [
            dot(jnp.concatenate(halves, axis=0), jnp.concatenate(chunks, axis=0), 0, 0, bf16),
            dot(jnp.concatenate(hiddens, axis=0), all_low, 0, 0, bf16),
            jnp.zeros((32, width), bf16),
        ],
        axis=0,
    )
    ffn_grads = lax.psum_scatter(ffn_grads, SEQ, scatter_dimension=0, tiled=True)
    ffn_grads = lax.all_gather(ffn_grads, SEQ, axis=0, tiled=True)
    gate_grad = ffn_grads[:ff].astype(f32).T
    up_grad = ffn_grads[ff : 2 * ff].astype(f32).T
    down_grad = ffn_grads[2 * ff : 3 * ff].astype(f32)

    block_a, block_b = plane_gather((residual + ffn).astype(bf16))
    shape = (TPS, own // 2, width)
    block_output = absolute_rows(
        jnp.concatenate(block_a, axis=0).reshape(shape),
        jnp.concatenate(block_b, axis=0).reshape(shape),
        to_a,
        to_b,
    )

    grad_rows = lax.dynamic_slice_in_dim(
        out_cotangent.reshape(count, width), place * own, own, axis=0
    )
    scaled = second_gain * d_normed2
    second_part = jnp.sum(d_normed2 * residual * inverse_two, axis=0)
    d_residual = grad_rows + inverse_two * (
        scaled
        - residual
        * inverse_two
        * inverse_two
        * jnp.mean(scaled * residual, axis=-1, keepdims=True)
    )
    d_low = d_residual.astype(bf16)

    out_abs = jnp.concatenate(
        [
            to_absolute(out_rel_a.reshape(RING, RING, half, width)),
            to_absolute(
                out_rel_b.reshape(RING, RING, half, width).transpose(1, 0, 2, 3)
            ),
        ],
        axis=2,
    ).reshape(TPS * chans, width)
    d_mixer = dot(d_low, out_abs, 1, 1)

    rows_n1 = lax.dynamic_slice_in_dim(normed1, place * own, own, axis=0)
    local_edge = lax.dynamic_slice_in_dim(normed1, place * own - 8, 8, axis=0)
    at_start = place % per_seq == 0
    edge_n1 = jnp.where(at_start, carried[place // per_seq], local_edge)
    again = dot(jnp.concatenate([edge_n1, rows_n1], axis=0), in_all, 1, 1)
    channels = TPS * chans
    b_all, c_all, x_all = (again[:, g * channels : (g + 1) * channels] for g in range(3))
    b_gate, c_gate, x_gate = b_all[8:], c_all[8:], x_all[8:]
    product = (b_all * x_all).astype(bf16).astype(f32)
    rows_one = lax.dynamic_slice_in_dim(one_back.reshape(count, 1), place * own, own, axis=0)
    rows_two = lax.dynamic_slice_in_dim(two_back.reshape(count, 1), place * own, own, axis=0)
    lagged_one = rows_one * product[7 : 7 + own]
    lagged_two = rows_two * product[6 : 6 + own]
    product = product[8:]
    convolved = taps[0] * product + taps[1] * lagged_one + taps[2] * lagged_two

    d_conv = d_mixer * c_gate
    d_cgate = d_mixer * convolved
    lag_one = rows_one * d_conv
    lag_two = rows_two * d_conv
    pairs = []
    for sq in range(8):
        for j in range(TPS):
            if j % per_seq:
                pairs.append((sq * TPS + j, sq * TPS + j - 1))
            elif sq:
                pairs.append((sq * TPS + j, (sq - 1) * TPS + j + per_seq - 1))
    edges = lax.ppermute(jnp.concatenate([lag_one[:2], lag_two[:2]], axis=0), ALL, pairs)
    ahead_one = jnp.concatenate([lag_one[1:], edges[:1]], axis=0)
    ahead_two = jnp.concatenate([lag_two[2:], edges[2:]], axis=0)
    d_product = taps[0] * d_conv + taps[1] * ahead_one + taps[2] * ahead_two
    d_projected = jnp.concatenate(
        [d_product * x_gate, d_cgate, d_product * b_gate], axis=1
    ).astype(bf16)
    d_normed1 = dot(d_projected, in_all, 1, 0)
    rows_inverse = lax.rsqrt(jnp.mean(rows_in * rows_in, axis=-1, keepdims=True) + epsilon)
    scaled_one = first_gain * d_normed1
    first_part = jnp.sum(d_normed1 * rows_in * rows_inverse, axis=0)
    input_rows = d_residual + rows_inverse * (
        scaled_one
        - rows_in
        * rows_inverse
        * rows_inverse
        * jnp.mean(scaled_one * rows_in, axis=-1, keepdims=True)
    )
    input_a, input_b = plane_gather(input_rows.astype(bf16))
    input_grad = absolute_rows(
        jnp.concatenate(input_a, axis=0).reshape(shape),
        jnp.concatenate(input_b, axis=0).reshape(shape),
        to_a,
        to_b,
    )

    small = jnp.stack(
        [
            first_part,
            second_part,
            jnp.sum(d_conv * product, axis=0),
            jnp.sum(d_conv * lagged_one, axis=0),
            jnp.sum(d_conv * lagged_two, axis=0),
        ],
        axis=0,
    )
    small = small + lax.ppermute(small, "core", [(0, 1), (1, 0)])
    small = ring_total(ring_total(ring_total(small, "z"), "y"), "x")
    first_grad, second_grad = small[0], small[1]
    taps_grad = lax.dynamic_slice_in_dim(small[2:], place * chans, chans, axis=1)

    out_part_a = dot(mixer_a, d_low, 1, 0, bf16)
    out_part_b = dot(mixer_b, d_low, 1, 0, bf16)
    step = RING * half
    out_part = plane_scatter(
        [out_part_a[step * k : step * (k + 1)] for k in range(RING)],
        [out_part_b[step * k : step * (k + 1)] for k in range(RING)],
    ).astype(bf16)
    blocks = d_projected.reshape(own, 3, RING, RING, chans).transpose(2, 3, 1, 4, 0)
    blocks = blocks.reshape(RING, RING, 3 * chans, own)
    received = to_absolute(plane_exchange(to_relative(blocks)))
    received = received.reshape(TPS, 3 * chans, own).transpose(1, 0, 2).reshape(3 * chans, count)
    in_part = dot(received, normed1, 1, 0, bf16)
    part = jnp.concatenate([in_part, out_part], axis=0)
    middle = part.shape[0] // 2
    low_half, high_half = part[:middle], part[middle:]
    is_low = lax.axis_index("core") == 0
    theirs = lax.ppermute(jnp.where(is_low, high_half, low_half), "core", [(0, 1), (1, 0)])
    mine = jnp.where(is_low, low_half, high_half).astype(f32) + theirs.astype(f32)
    mine = ring_total(mine.astype(bf16), "z").astype(bf16)
    theirs = lax.ppermute(mine, "core", [(0, 1), (1, 0)])
    total = jnp.concatenate(
        [jnp.where(is_low, mine, theirs), jnp.where(is_low, theirs, mine)], axis=0
    ).astype(f32)
    in_grad = total[: 3 * chans].reshape(3, chans, width).transpose(2, 0, 1)
    out_grad = total[3 * chans :]

    return (
        block_output.reshape(seqs, seg, width),
        input_grad.reshape(seqs, seg, width),
        first_grad,
        in_grad,
        taps_grad,
        out_grad,
        second_grad,
        gate_grad,
        up_grad,
        down_grad,
    )


def solution(mesh):
    grid = Mesh(mesh.devices.reshape(4, 2, RING, RING), ALL)
    return jax.shard_map(
        shards,
        mesh=grid,
        in_specs=(
            P(None, SEQ, None),
            P(),
            P(None, None, TP),
            P(None, TP),
            P(TP, None),
            P(),
            P(None, TP),
            P(None, TP),
            P(TP, None),
            P(),
            P(None, SEQ, None),
        ),
        out_specs=(
            P(None, SEQ, None),
            P(None, SEQ, None),
            P(),
            P(None, None, TP),
            P(None, TP),
            P(TP, None),
            P(),
            P(None, TP),
            P(None, TP),
            P(TP, None),
        ),
        check_vma=False,
    )
```

time: 592 us -> 548 us (0.926)
  the two profiles are of different devices: /device:TPU:65 before, /device:TPU:6 now
where the time goes in v1:
time: 548 us; the launch traced here: 539 us
  starting transfers between devices  188 us (34%)
  waiting for transfers between devices  157 us (29%)
  local copies, waits for them, and re-layouts  54.8 us (10%)
  other arithmetic  48.8 us (9%)
  matrix products  37.2 us (7%)
  Pallas kernels  35.2 us (6%)
  between operations  19.1 us (3%)
    ppermute x128, starting transfers between devices, turn(): lax.ppermute(value, axis, [(i, (i + steps) % RING) for i in range(RING)])  183 us
    ppermute x128, waiting for transfers between devices, turn(): lax.ppermute(value, axis, [(i, (i + steps) % RING) for i in range(RING)])  155 us
    dot_general x46, matrix products, dot(): lax.dot_general(left, right, (((left_dim,), (right_dim,)), ((), ())), pre...  37.2 us
    unnamed x251, local copies, waits for them, and re-layouts  26.2 us
    pallas_call x2, Pallas kernels, absolute_rows(): pl.pallas_call(body, grid_spec=pltpu.PrefetchScalarGridSpec(num_scalar_pr...  23.7 us
    pallas_call x1, Pallas kernels, relative_rows(): pl.pallas_call(body, grid_spec=pltpu.PrefetchScalarGridSpec(num_scalar_pr...  11.5 us
  transfers between devices with their start and end apart: 136, of which 56 were waited for; matrix products, arithmetic and copies ran while one was open for 19% of the time, Pallas kernels for 7%

profile of v1, /device:TPU:6, one launch (start us, length us, event | category | flops | bytes accessed | tf_op | source)
XLA Modules:
  0.0 539.4 jit_solution(13769733930453280700)
XLA Ops:
  9.6 3.0 collective-permute-start.14
  14.3 4.2 multiply_reduce_fusion
  26.3 3.9 multiply_convert_fusion.1
  34.8 11.5 %relative_rows.1 = (bf16[16,64,1024]{2,1,0:T(8,128)(2,1)}, bf16[16,64,1024]{2,1,0:T(8,128)(2,1)}) custom-call(s32[16]{0:T(128)} %get-tuple-element.173.ia, s32[16]{0:T(128)} %get-tuple-element.174.ib, f32[32,64,1024]{2,1,0:T(8,128)} %bitcast.271, f32[32,64,1024]{2,1,0:T(8,128)} %bitcast.272), custom_call_target="tpu_custom_call" | custom-call | tf_op jit(solution)/shard_map/relative_rows/pallas_call | solution.py:119
  46.4 3.0 fusion.120
  62.5 2.4 collective-permute-start.3
  65.0 3.2 collective-permute-start.18
  74.4 3.7 collective-permute-start.10
  81.0 4.7 collective-permute-done.11
  85.8 3.7 collective-permute-start.13
  94.0 3.1 collective-permute-start.22
  97.5 2.7 collective-permute-done.21
  102.5 3.7 collective-permute-start.24
  108.6 10.9 %collective-permute-done.25 = bf16[256,1024]{1,0:T(8,128)(2,1)S(1)} collective-permute-done((bf16[256,1024]{1,0:T(8,128)(2,1)S(1)}, bf16[256,1024]{1,0:T(8,128)(2,1)S(1)}, u32[]{:S(2)}, u32[]{:S(2)}) %collective-permute-start.25) | collective-permute-done | bytes 524320 | tf_op jit(solution)/shard_map/ppermute | solution.py:20
  119.6 3.3 collective-permute-start.27
  126.2 3.1 collective-permute-done.26
  134.5 3.1 collective-permute-done.36
  139.1 2.8 collective-permute-start.39
  143.7 5.4 %collective-permute-done.39 = bf16[256,1024]{1,0:T(8,128)(2,1)S(1)} collective-permute-done((bf16[256,1024]{1,0:T(8,128)(2,1)S(1)}, bf16[256,1024]{1,0:T(8,128)(2,1)S(1)}, u32[]{:S(2)}, u32[]{:S(2)}) %collective-permute-start.39) | collective-permute-done | bytes 524320 | tf_op jit(solution)/shard_map/ppermute | solution.py:20
  149.2 3.8 collective-permute-start.40
  156.8 4.0 collective-permute-done.41
  163.4 2.6 convolution_convert_fusion
  197.9 3.0 collective-permute-start.30
  201.0 3.2 collective-permute-start.65
  208.5 3.8 collective-permute-start.31
  214.2 3.5 collective-permute-start.66
  227.5 3.3 collective-permute-start.68
  240.9 2.9 collective-permute-done.69
  243.9 8.3 %collective-permute-done.70 = bf16[128,1024]{1,0:T(8,128)(2,1)S(1)} collective-permute-done((bf16[128,1024]{1,0:T(8,128)(2,1)S(1)}, bf16[128,1024]{1,0:T(8,128)(2,1)S(1)}, u32[]{:S(2)}, u32[]{:S(2)}) %collective-permute-start.70) | collective-permute-done | bytes 262176 | tf_op jit(solution)/shard_map/ppermute | solution.py:20
  252.3 2.5 collective-permute-start.71
  255.2 3.3 collective-permute-start.43
  258.6 4.7 collective-permute-done.71
  263.3 3.8 collective-permute-done.73
  267.5 4.8 collective-permute-start.75
  274.7 3.2 collective-permute-start.47
  279.4 3.8 collective-permute-done.47
  286.3 3.6 collective-permute-start.56
  291.2 2.7 collective-permute-start.114
  295.0 3.9 collective-permute-done.114
  304.6 2.4 collective-permute-start.51
  314.4 2.6 collective-permute-start.117
  330.3 2.8 collective-permute-start.52
  336.4 10.9 %collective-permute-done.125 = bf16[32,1024]{1,0:T(8,128)(2,1)S(1)} collective-permute-done((bf16[32,1024]{1,0:T(8,128)(2,1)S(1)}, bf16[32,1024]{1,0:T(8,128)(2,1)S(1)}, u32[]{:S(2)}, u32[]{:S(2)}) %collective-permute-start.125) | collective-permute-done | bytes 65568 | tf_op jit(solution)/shard_map/ppermute | solution.py:20
  349.6 3.5 collective-permute-done.126
  353.1 3.4 collective-permute-start.61
  356.8 3.5 collective-permute-start.55
  368.1 11.8 %absolute_rows.2 = f32[16,128,1024]{2,1,0:T(8,128)} custom-call(s32[16]{0:T(128)} %get-tuple-element.176.ia, s32[16]{0:T(128)} %get-tuple-element.175.ib, bf16[16,64,1024]{2,1,0:T(8,128)(2,1)} %bitcast.37.top, bf16[16,64,1024]{2,1,0:T(8,128)(2,1)} %bitcast.38.bottom), custom_call_target="tpu_custom_call" | custom-call | tf_op jit(solution)/shard_map/absolute_rows/pallas_call | solution.py:143
  379.9 3.5 copy.128
  391.4 3.4 slice_convert_fusion
  402.7 4.1 multiply_reduce_fusion.5
  412.4 2.9 collective-permute-start.100
  417.2 3.6 collective-permute-done.101
  420.8 3.6 collective-permute-start.102
  429.8 4.5 collective-permute-start.105
  434.7 2.8 collective-permute-start.107
  442.5 2.4 collective-permute-start.86
  453.6 2.5 collective-permute-start.95
  461.6 10.1 %collective-permute-done.111 = bf16[4,192,128]{2,1,0:T(8,128)(2,1)S(1)} collective-permute-done((bf16[4,192,128]{2,1,0:T(8,128)(2,1)S(1)}, bf16[4,192,128]{2,1,0:T(8,128)(2,1)S(1)}, u32[]{:S(2)}, u32[]{:S(2)}) %collective-permute-start.111) | collective-permute-done | bytes 196640 | tf_op jit(solution)/shard_map/ppermute | solution.py:20
  473.3 5.7 %collective-permute-done.112 = bf16[4,192,128]{2,1,0:T(8,128)(2,1)S(1)} collective-permute-done((bf16[4,192,128]{2,1,0:T(8,128)(2,1)S(1)}, bf16[4,192,128]{2,1,0:T(8,128)(2,1)S(1)}, u32[]{:S(2)}, u32[]{:S(2)}) %collective-permute-start.112) | collective-permute-done | bytes 196640 | tf_op jit(solution)/shard_map/ppermute | solution.py:20
  479.0 6.8 %collective-permute-done.113 = bf16[4,192,128]{2,1,0:T(8,128)(2,1)S(1)} collective-permute-done((bf16[4,192,128]{2,1,0:T(8,128)(2,1)S(1)}, bf16[4,192,128]{2,1,0:T(8,128)(2,1)S(1)}, u32[]{:S(2)}, u32[]{:S(2)}) %collective-permute-start.113) | collective-permute-done | bytes 196640 | tf_op jit(solution)/shard_map/ppermute | solution.py:20
  498.1 3.5 collective-permute-done.129
  501.6 6.0 %collective-permute-done.130 = bf16[128,1024]{1,0:T(8,128)(2,1)S(1)} collective-permute-done((bf16[128,1024]{1,0:T(8,128)(2,1)S(1)}, bf16[128,1024]{1,0:T(8,128)(2,1)S(1)}, u32[]{:S(2)}, u32[]{:S(2)}) %collective-permute-start.130) | collective-permute-done | bytes 262176 | tf_op jit(solution)/shard_map/ppermute | solution.py:20
  509.6 5.6 %collective-permute-done.90 = bf16[128,1024]{1,0:T(8,128)(2,1)S(1)} collective-permute-done((bf16[128,1024]{1,0:T(8,128)(2,1)S(1)}, bf16[128,1024]{1,0:T(8,128)(2,1)S(1)}, u32[]{:S(2)}, u32[]{:S(2)}) %collective-permute-start.90) | collective-permute-done | bytes 262176 | tf_op jit(solution)/shard_map/ppermute | solution.py:20
  517.9 11.8 %absolute_rows.3 = f32[16,128,1024]{2,1,0:T(8,128)} custom-call(s32[16]{0:T(128)} %get-tuple-element.176.ia, s32[16]{0:T(128)} %get-tuple-element.175.ib, bf16[16,64,1024]{2,1,0:T(8,128)(2,1)} %bitcast.284, bf16[16,64,1024]{2,1,0:T(8,128)(2,1)} %bitcast.285), custom_call_target="tpu_custom_call" | custom-call | tf_op jit(solution)/shard_map/absolute_rows/pallas_call | solution.py:143
  (719 shorter events, 240.4 us)
Async XLA Ops:
  8.0 318.5 %reduce-scatter.2.cloned.1.call-start = ((), (), s32[]{:S(2)}) async-start(), calls=%async_computation.1 | async-start | bytes 2064384 | tf_op jit(solution)/shard_map/reduce_scatter | solution.py:279
  9.6 46.5 %collective-permute-start.14 = (bf16[32,1024]{1,0:T(8,128)(2,1)}, bf16[32,1024]{1,0:T(8,128)(2,1)S(1)}, u32[]{:S(2)}, u32[]{:S(2)}) collective-permute-start(bf16[32,1024]{1,0:T(8,128)(2,1)} %get-tuple-element.150), channel_id=1, source_target_pairs={{0,12},{4,0},{8,4},{12,8},{1,13},{5,1},{9,5},{13,9},{2,14},{6,2},{... | collective-permute-start | bytes 196616 | tf_op jit(solution)/shard_map/ppermute | solution.py:20
  12.7 45.7 %collective-permute-start.15 = (bf16[32,1024]{1,0:T(8,128)(2,1)}, bf16[32,1024]{1,0:T(8,128)(2,1)S(1)}, u32[]{:S(2)}, u32[]{:S(2)}) collective-permute-start(bf16[32,1024]{1,0:T(8,128)(2,1)} %get-tuple-element.150), channel_id=1, source_target_pairs={{0,8},{4,12},{8,0},{12,4},{1,9},{5,13},{9,1},{13,5},{2,10},{6,14},... | collective-permute-start | bytes 196616 | tf_op jit(solution)/shard_map/ppermute | solution.py:20
  13.3 45.2 %collective-permute-start.16 = (bf16[32,1024]{1,0:T(8,128)(2,1)}, bf16[32,1024]{1,0:T(8,128)(2,1)}, u32[]{:S(2)}, u32[]{:S(2)}) collective-permute-start(bf16[32,1024]{1,0:T(8,128)(2,1)} %get-tuple-element.150), channel_id=1, source_target_pairs={{0,4},{4,8},{8,12},{12,0},{1,5},{5,9},{9,13},{13,1},{2,6},{6,10},{... | collective-permute-start | bytes 196616 | tf_op jit(solution)/shard_map/ppermute | solution.py:20
  23.6 27.3 %collective-permute-start = (bf16[2,8,1024]{2,1,0:T(8,128)(2,1)}, bf16[2,8,1024]{2,1,0:T(8,128)(2,1)}, u32[]{:S(2)}, u32[]{:S(2)}) collective-permute-start(bf16[2,8,1024]{2,1,0:T(8,128)(2,1)} %slice.776), channel_id=1, source_target_pairs={{0,16},{1,17},{2,18},{3,19},{4,20},{5,21},{6,22},{7,23},{8,24},{9,... | collective-permute-start | bytes 98312 | tf_op jit(solution)/shard_map/ppermute | solution.py:218
  25.4 37.1 %collective-permute-start.7 = (bf16[32,1024]{1,0:T(8,128)(2,1)}, bf16[32,1024]{1,0:T(8,128)(2,1)S(1)}, u32[]{:S(2)}, u32[]{:S(2)}) collective-permute-start(bf16[32,1024]{1,0:T(8,128)(2,1)} %get-tuple-element.147), channel_id=1, source_target_pairs={{0,3},{1,0},{2,1},{3,2},{4,7},{5,4},{6,5},{7,6},{8,11},{9,8},{10,9... | collective-permute-start | bytes 196616 | tf_op jit(solution)/shard_map/ppermute | solution.py:20
  50.8 14.1 %collective-permute-start.8 = (bf16[32,1024]{1,0:T(8,128)(2,1)}, bf16[32,1024]{1,0:T(8,128)(2,1)S(1)}, u32[]{:S(2)}, u32[]{:S(2)}) collective-permute-start(bf16[32,1024]{1,0:T(8,128)(2,1)} %get-tuple-element.147), channel_id=1, source_target_pairs={{0,2},{1,3},{2,0},{3,1},{4,6},{5,7},{6,4},{7,5},{8,10},{9,11},{10,... | collective-permute-start | bytes 196616 | tf_op jit(solution)/shard_map/ppermute | solution.py:20
  58.3 10.8 %collective-permute-start.1 = (bf16[4,64,128]{2,1,0:T(8,128)(2,1)S(1)}, bf16[4,64,128]{2,1,0:T(8,128)(2,1)S(1)}, u32[]{:S(2)}, u32[]{:S(2)}) collective-permute-start(bf16[4,64,128]{2,1,0:T(8,128)(2,1)S(1)} %get-tuple-element.146), channel_id=1, source_target_pairs={{0,3},{1,0},{2,1},{3,2},{4,7},{5,4},{6,5},{7,6},{8,11},{9,8},{10,9... | collective-permute-start | bytes 196616 | tf_op jit(solution)/shard_map/ppermute | solution.py:20
  64.9 15.7 %collective-permute-start.17 = (bf16[128,1024]{1,0:T(8,128)(2,1)S(1)}, bf16[128,1024]{1,0:T(8,128)(2,1)S(1)}, u32[]{:S(2)}, u32[]{:S(2)}) collective-permute-start(bf16[128,1024]{1,0:T(8,128)(2,1)S(1)} %pad_maximum_fusion.32), channel_id=1, source_target_pairs={{0,3},{1,0},{2,1},{3,2},{4,7},{5,4},{6,5},{7,6},{8,11},{9,8},{10,9... | collective-permute-start | bytes 786440 | tf_op jit(solution)/shard_map/ppermute | solution.py:20
  65.0 13.8 %collective-permute-start.18 = (bf16[128,1024]{1,0:T(8,128)(2,1)S(1)}, bf16[128,1024]{1,0:T(8,128)(2,1)S(1)}, u32[]{:S(2)}, u32[]{:S(2)}) collective-permute-start(bf16[128,1024]{1,0:T(8,128)(2,1)S(1)} %pad_maximum_fusion.32), channel_id=1, source_target_pairs={{0,1},{1,2},{2,3},{3,0},{4,5},{5,6},{6,7},{7,4},{8,9},{9,10},{10,1... | collective-permute-start | bytes 786440 | tf_op jit(solution)/shard_map/ppermute | solution.py:20
  74.4 11.3 %collective-permute-start.10 = (bf16[128,1024]{1,0:T(8,128)(2,1)S(1)}, bf16[128,1024]{1,0:T(8,128)(2,1)S(1)}, u32[]{:S(2)}, u32[]{:S(2)}) collective-permute-start(bf16[128,1024]{1,0:T(8,128)(2,1)S(1)} %pad_maximum_fusion.31), channel_id=1, source_target_pairs={{0,12},{4,0},{8,4},{12,8},{1,13},{5,1},{9,5},{13,9},{2,14},{6,2},{... | collective-permute-start | bytes 786440 | tf_op jit(solution)/shard_map/ppermute | solution.py:20
  102.5 17.0 %collective-permute-start.24 = (bf16[256,1024]{1,0:T(8,128)(2,1)S(1)}, bf16[256,1024]{1,0:T(8,128)(2,1)S(1)}, u32[]{:S(2)}, u32[]{:S(2)}) collective-permute-start(bf16[256,1024]{1,0:T(8,128)(2,1)S(1)} %pad_maximum_fusion.3), channel_id=1, source_target_pairs={{0,12},{4,0},{8,4},{12,8},{1,13},{5,1},{9,5},{13,9},{2,14},{6,2},{... | collective-permute-start | bytes 1572872 | tf_op jit(solution)/shard_map/ppermute | solution.py:20
  106.2 13.2 %collective-permute-start.25 = (bf16[256,1024]{1,0:T(8,128)(2,1)S(1)}, bf16[256,1024]{1,0:T(8,128)(2,1)S(1)}, u32[]{:S(2)}, u32[]{:S(2)}) collective-permute-start(bf16[256,1024]{1,0:T(8,128)(2,1)S(1)} %pad_maximum_fusion.3), channel_id=1, source_target_pairs={{0,4},{4,8},{8,12},{12,0},{1,5},{5,9},{9,13},{13,1},{2,6},{6,10},{... | collective-permute-start | bytes 1572872 | tf_op jit(solution)/shard_map/ppermute | solution.py:20
  138.6 14.3 %collective-permute-start.38 = (bf16[256,1024]{1,0:T(8,128)(2,1)S(1)}, bf16[256,1024]{1,0:T(8,128)(2,1)S(1)}, u32[]{:S(2)}, u32[]{:S(2)}) collective-permute-start(bf16[256,1024]{1,0:T(8,128)(2,1)S(1)} %pad_maximum_fusion.6), channel_id=1, source_target_pairs={{0,3},{1,0},{2,1},{3,2},{4,7},{5,4},{6,5},{7,6},{8,11},{9,8},{10,9... | collective-permute-start | bytes 1572872 | tf_op jit(solution)/shard_map/ppermute | solution.py:20
  169.1 210.8 %all-gather.6.cloned.1.call-start = ((), (), s32[]{:S(2)}) async-start(), calls=%async_computation.3 | async-start | bytes 6340608 | tf_op jit(solution)/shard_map/all_gather | solution.py:207
  173.9 217.5 %all-gather.4.cloned.1.call-start = ((), (), s32[]{:S(2)}) async-start(), calls=%async_computation.2 | async-start | bytes 2064384 | tf_op jit(solution)/shard_map/all_gather | solution.py:280
  201.0 12.9 %collective-permute-start.63 = (bf16[128,1024]{1,0:T(8,128)(2,1)S(1)}, bf16[128,1024]{1,0:T(8,128)(2,1)S(1)}, u32[]{:S(2)}, u32[]{:S(2)}) collective-permute-start(bf16[128,1024]{1,0:T(8,128)(2,1)S(1)} %get-tuple-element.102), channel_id=1, source_target_pairs={{0,4},{4,8},{8,12},{12,0},{1,5},{5,9},{9,13},{13,1},{2,6},{6,10},{... | collective-permute-start | bytes 786440 | tf_op jit(solution)/shard_map/ppermute | solution.py:20
  201.0 13.0 %collective-permute-start.65 = (bf16[128,1024]{1,0:T(8,128)(2,1)S(1)}, bf16[128,1024]{1,0:T(8,128)(2,1)S(1)}, u32[]{:S(2)}, u32[]{:S(2)}) collective-permute-start(bf16[128,1024]{1,0:T(8,128)(2,1)S(1)} %get-tuple-element.103), channel_id=1, source_target_pairs={{0,12},{4,0},{8,4},{12,8},{1,13},{5,1},{9,5},{13,9},{2,14},{6,2},{... | collective-permute-start | bytes 786440 | tf_op jit(solution)/shard_map/ppermute | solution.py:20
  207.7 12.5 %collective-permute-start.29 = (bf16[256,1024]{1,0:T(8,128)(2,1)S(1)}, bf16[256,1024]{1,0:T(8,128)(2,1)S(1)}, u32[]{:S(2)}, u32[]{:S(2)}) collective-permute-start(bf16[256,1024]{1,0:T(8,128)(2,1)S(1)} %pad_maximum_fusion.4), channel_id=1, source_target_pairs={{0,4},{4,8},{8,12},{12,0},{1,5},{5,9},{9,13},{13,1},{2,6},{6,10},{... | collective-permute-start | bytes 1572872 | tf_op jit(solution)/shard_map/ppermute | solution.py:20
  208.5 11.7 %collective-permute-start.31 = (bf16[256,1024]{1,0:T(8,128)(2,1)S(1)}, bf16[256,1024]{1,0:T(8,128)(2,1)S(1)}, u32[]{:S(2)}, u32[]{:S(2)}) collective-permute-start(bf16[256,1024]{1,0:T(8,128)(2,1)S(1)} %pad_maximum_fusion.5), channel_id=1, source_target_pairs={{0,12},{4,0},{8,4},{12,8},{1,13},{5,1},{9,5},{13,9},{2,14},{6,2},{... | collective-permute-start | bytes 1572872 | tf_op jit(solution)/shard_map/ppermute | solution.py:20
  214.0 11.9 %collective-permute-start.64 = (bf16[256,1024]{1,0:T(8,128)(2,1)S(1)}, bf16[256,1024]{1,0:T(8,128)(2,1)S(1)}, u32[]{:S(2)}, u32[]{:S(2)}) collective-permute-start(bf16[256,1024]{1,0:T(8,128)(2,1)S(1)} %pad_maximum_fusion.11), channel_id=1, source_target_pairs={{0,4},{4,8},{8,12},{12,0},{1,5},{5,9},{9,13},{13,1},{2,6},{6,10},{... | collective-permute-start | bytes 1572872 | tf_op jit(solution)/shard_map/ppermute | solution.py:20
  214.2 11.7 %collective-permute-start.66 = (bf16[256,1024]{1,0:T(8,128)(2,1)S(1)}, bf16[256,1024]{1,0:T(8,128)(2,1)S(1)}, u32[]{:S(2)}, u32[]{:S(2)}) collective-permute-start(bf16[256,1024]{1,0:T(8,128)(2,1)S(1)} %pad_maximum_fusion.12), channel_id=1, source_target_pairs={{0,12},{4,0},{8,4},{12,8},{1,13},{5,1},{9,5},{13,9},{2,14},{6,2},{... | collective-permute-start | bytes 1572872 | tf_op jit(solution)/shard_map/ppermute | solution.py:20
  220.5 12.3 %collective-permute-start.32 = (bf16[64,1024]{1,0:T(8,128)(2,1)S(1)}, bf16[64,1024]{1,0:T(8,128)(2,1)S(1)}, u32[]{:S(2)}, u32[]{:S(2)}) collective-permute-start(bf16[64,1024]{1,0:T(8,128)(2,1)S(1)} %get-tuple-element.109), channel_id=1, source_target_pairs={{0,1},{1,2},{2,3},{3,0},{4,5},{5,6},{6,7},{7,4},{8,9},{9,10},{10,1... | collective-permute-start | bytes 393224 | tf_op jit(solution)/shard_map/ppermute | solution.py:20
  221.4 12.8 %collective-permute-start.33 = (bf16[64,1024]{1,0:T(8,128)(2,1)S(1)}, bf16[64,1024]{1,0:T(8,128)(2,1)S(1)}, u32[]{:S(2)}, u32[]{:S(2)}) collective-permute-start(bf16[64,1024]{1,0:T(8,128)(2,1)S(1)} %get-tuple-element.111), channel_id=1, source_target_pairs={{0,2},{1,3},{2,0},{3,1},{4,6},{5,7},{6,4},{7,5},{8,10},{9,11},{10,... | collective-permute-start | bytes 393224 | tf_op jit(solution)/shard_map/ppermute | solution.py:20
  223.5 12.6 %collective-permute-start.34 = (bf16[64,1024]{1,0:T(8,128)(2,1)S(1)}, bf16[64,1024]{1,0:T(8,128)(2,1)S(1)}, u32[]{:S(2)}, u32[]{:S(2)}) collective-permute-start(bf16[64,1024]{1,0:T(8,128)(2,1)S(1)} %get-tuple-element.110), channel_id=1, source_target_pairs={{0,3},{1,0},{2,1},{3,2},{4,7},{5,4},{6,5},{7,6},{8,11},{9,8},{10,9... | collective-permute-start | bytes 393224 | tf_op jit(solution)/shard_map/ppermute | solution.py:20
  226.1 11.4 %collective-permute-start.67 = (bf16[64,1024]{1,0:T(8,128)(2,1)S(1)}, bf16[64,1024]{1,0:T(8,128)(2,1)S(1)}, u32[]{:S(2)}, u32[]{:S(2)}) collective-permute-start(bf16[64,1024]{1,0:T(8,128)(2,1)S(1)} %get-tuple-element.99), channel_id=1, source_target_pairs={{0,1},{1,2},{2,3},{3,0},{4,5},{5,6},{6,7},{7,4},{8,9},{9,10},{10,1... | collective-permute-start | bytes 393224 | tf_op jit(solution)/shard_map/ppermute | solution.py:20
  227.5 12.9 %collective-permute-start.68 = (bf16[64,1024]{1,0:T(8,128)(2,1)S(1)}, bf16[64,1024]{1,0:T(8,128)(2,1)S(1)}, u32[]{:S(2)}, u32[]{:S(2)}) collective-permute-start(bf16[64,1024]{1,0:T(8,128)(2,1)S(1)} %get-tuple-element.101), channel_id=1, source_target_pairs={{0,2},{1,3},{2,0},{3,1},{4,6},{5,7},{6,4},{7,5},{8,10},{9,11},{10,... | collective-permute-start | bytes 393224 | tf_op jit(solution)/shard_map/ppermute | solution.py:20
  232.8 11.0 %collective-permute-start.69 = (bf16[64,1024]{1,0:T(8,128)(2,1)S(1)}, bf16[64,1024]{1,0:T(8,128)(2,1)S(1)}, u32[]{:S(2)}, u32[]{:S(2)}) collective-permute-start(bf16[64,1024]{1,0:T(8,128)(2,1)S(1)} %get-tuple-element.100), channel_id=1, source_target_pairs={{0,3},{1,0},{2,1},{3,2},{4,7},{5,4},{6,5},{7,6},{8,11},{9,8},{10,9... | collective-permute-start | bytes 393224 | tf_op jit(solution)/shard_map/ppermute | solution.py:20
  234.2 20.8 %collective-permute-start.42 = (bf16[128,1024]{1,0:T(8,128)(2,1)S(1)}, bf16[128,1024]{1,0:T(8,128)(2,1)S(1)}, u32[]{:S(2)}, u32[]{:S(2)}) collective-permute-start(bf16[128,1024]{1,0:T(8,128)(2,1)S(1)} %get-tuple-element.117), channel_id=1, source_target_pairs={{0,1},{1,2},{2,3},{3,0},{4,5},{5,6},{6,7},{7,4},{8,9},{9,10},{10,1... | collective-permute-start | bytes 786440 | tf_op jit(solution)/shard_map/ppermute | solution.py:20
  236.1 16.1 %collective-permute-start.70 = (bf16[128,1024]{1,0:T(8,128)(2,1)S(1)}, bf16[128,1024]{1,0:T(8,128)(2,1)S(1)}, u32[]{:S(2)}, u32[]{:S(2)}) collective-permute-start(bf16[128,1024]{1,0:T(8,128)(2,1)S(1)} %get-tuple-element.107), channel_id=1, source_target_pairs={{0,1},{1,2},{2,3},{3,0},{4,5},{5,6},{6,7},{7,4},{8,9},{9,10},{10,1... | collective-permute-start | bytes 786440 | tf_op jit(solution)/shard_map/ppermute | solution.py:20
  237.6 20.9 %collective-permute-start.44 = (bf16[128,1024]{1,0:T(8,128)(2,1)S(1)}, bf16[128,1024]{1,0:T(8,128)(2,1)S(1)}, u32[]{:S(2)}, u32[]{:S(2)}) collective-permute-start(bf16[128,1024]{1,0:T(8,128)(2,1)S(1)} %get-tuple-element.118), channel_id=1, source_target_pairs={{0,3},{1,0},{2,1},{3,2},{4,7},{5,4},{6,5},{7,6},{8,11},{9,8},{10,9... | collective-permute-start | bytes 786440 | tf_op jit(solution)/shard_map/ppermute | solution.py:20
  240.5 14.4 %collective-permute-start.72 = (bf16[128,1024]{1,0:T(8,128)(2,1)S(1)}, bf16[128,1024]{1,0:T(8,128)(2,1)S(1)}, u32[]{:S(2)}, u32[]{:S(2)}) collective-permute-start(bf16[128,1024]{1,0:T(8,128)(2,1)S(1)} %get-tuple-element.108), channel_id=1, source_target_pairs={{0,3},{1,0},{2,1},{3,2},{4,7},{5,4},{6,5},{7,6},{8,11},{9,8},{10,9... | collective-permute-start | bytes 786440 | tf_op jit(solution)/shard_map/ppermute | solution.py:20
  252.3 11.0 %collective-permute-start.71 = (bf16[256,1024]{1,0:T(8,128)(2,1)S(1)}, bf16[256,1024]{1,0:T(8,128)(2,1)S(1)}, u32[]{:S(2)}, u32[]{:S(2)}) collective-permute-start(bf16[256,1024]{1,0:T(8,128)(2,1)S(1)} %pad_maximum_fusion.13), channel_id=1, source_target_pairs={{0,1},{1,2},{2,3},{3,0},{4,5},{5,6},{6,7},{7,4},{8,9},{9,10},{10,1... | collective-permute-start | bytes 1572872 | tf_op jit(solution)/shard_map/ppermute | solution.py:20
  254.9 12.2 %collective-permute-start.73 = (bf16[256,1024]{1,0:T(8,128)(2,1)S(1)}, bf16[256,1024]{1,0:T(8,128)(2,1)S(1)}, u32[]{:S(2)}, u32[]{:S(2)}) collective-permute-start(bf16[256,1024]{1,0:T(8,128)(2,1)S(1)} %pad_maximum_fusion.14), channel_id=1, source_target_pairs={{0,3},{1,0},{2,1},{3,2},{4,7},{5,4},{6,5},{7,6},{8,11},{9,8},{10,9... | collective-permute-start | bytes 1572872 | tf_op jit(solution)/shard_map/ppermute | solution.py:20
  255.2 17.1 %collective-permute-start.43 = (bf16[256,1024]{1,0:T(8,128)(2,1)S(1)}, bf16[256,1024]{1,0:T(8,128)(2,1)S(1)}, u32[]{:S(2)}, u32[]{:S(2)}) collective-permute-start(bf16[256,1024]{1,0:T(8,128)(2,1)S(1)} %pad_maximum_fusion.7), channel_id=1, source_target_pairs={{0,1},{1,2},{2,3},{3,0},{4,5},{5,6},{6,7},{7,4},{8,9},{9,10},{10,1... | collective-permute-start | bytes 1572872 | tf_op jit(solution)/shard_map/ppermute | solution.py:20
  258.6 14.2 %collective-permute-start.45 = (bf16[256,1024]{1,0:T(8,128)(2,1)S(1)}, bf16[256,1024]{1,0:T(8,128)(2,1)S(1)}, u32[]{:S(2)}, u32[]{:S(2)}) collective-permute-start(bf16[256,1024]{1,0:T(8,128)(2,1)S(1)} %pad_maximum_fusion.8), channel_id=1, source_target_pairs={{0,3},{1,0},{2,1},{3,2},{4,7},{5,4},{6,5},{7,6},{8,11},{9,8},{10,9... | collective-permute-start | bytes 1572872 | tf_op jit(solution)/shard_map/ppermute | solution.py:20
  286.3 14.1 %collective-permute-start.56 = (bf16[64,1024]{1,0:T(8,128)(2,1)S(1)}, bf16[64,1024]{1,0:T(8,128)(2,1)S(1)}, u32[]{:S(2)}, u32[]{:S(2)}) collective-permute-start(bf16[64,1024]{1,0:T(8,128)(2,1)S(1)} %get-tuple-element.133), channel_id=1, source_target_pairs={{0,12},{4,0},{8,4},{12,8},{1,13},{5,1},{9,5},{13,9},{2,14},{6,2},{... | collective-permute-start | bytes 393224 | tf_op jit(solution)/shard_map/ppermute | solution.py:20
  289.9 13.2 %collective-permute-start.57 = (bf16[64,1024]{1,0:T(8,128)(2,1)S(1)}, bf16[64,1024]{1,0:T(8,128)(2,1)S(1)}, u32[]{:S(2)}, u32[]{:S(2)}) collective-permute-start(bf16[64,1024]{1,0:T(8,128)(2,1)S(1)} %get-tuple-element.133), channel_id=1, source_target_pairs={{0,8},{4,12},{8,0},{12,4},{1,9},{5,13},{9,1},{13,5},{2,10},{6,14},... | collective-permute-start | bytes 393224 | tf_op jit(solution)/shard_map/ppermute | solution.py:20
  289.9 14.8 %collective-permute-start.58 = (bf16[64,1024]{1,0:T(8,128)(2,1)S(1)}, bf16[64,1024]{1,0:T(8,128)(2,1)S(1)}, u32[]{:S(2)}, u32[]{:S(2)}) collective-permute-start(bf16[64,1024]{1,0:T(8,128)(2,1)S(1)} %get-tuple-element.133), channel_id=1, source_target_pairs={{0,4},{4,8},{8,12},{12,0},{1,5},{5,9},{9,13},{13,1},{2,6},{6,10},{... | collective-permute-start | bytes 393224 | tf_op jit(solution)/shard_map/ppermute | solution.py:20
  298.9 13.4 %collective-permute-start.49 = (bf16[64,1024]{1,0:T(8,128)(2,1)S(1)}, bf16[64,1024]{1,0:T(8,128)(2,1)S(1)}, u32[]{:S(2)}, u32[]{:S(2)}) collective-permute-start(bf16[64,1024]{1,0:T(8,128)(2,1)S(1)} %get-tuple-element.136), channel_id=1, source_target_pairs={{0,3},{1,0},{2,1},{3,2},{4,7},{5,4},{6,5},{7,6},{8,11},{9,8},{10,9... | collective-permute-start | bytes 393224 | tf_op jit(solution)/shard_map/ppermute | solution.py:20
  298.9 15.5 %collective-permute-start.50 = (bf16[64,1024]{1,0:T(8,128)(2,1)S(1)}, bf16[64,1024]{1,0:T(8,128)(2,1)S(1)}, u32[]{:S(2)}, u32[]{:S(2)}) collective-permute-start(bf16[64,1024]{1,0:T(8,128)(2,1)S(1)} %get-tuple-element.136), channel_id=1, source_target_pairs={{0,2},{1,3},{2,0},{3,1},{4,6},{5,7},{6,4},{7,5},{8,10},{9,11},{10,... | collective-permute-start | bytes 393224 | tf_op jit(solution)/shard_map/ppermute | solution.py:20
  304.6 13.7 %collective-permute-start.51 = (bf16[64,1024]{1,0:T(8,128)(2,1)S(1)}, bf16[64,1024]{1,0:T(8,128)(2,1)S(1)}, u32[]{:S(2)}, u32[]{:S(2)}) collective-permute-start(bf16[64,1024]{1,0:T(8,128)(2,1)S(1)} %get-tuple-element.136), channel_id=1, source_target_pairs={{0,1},{1,2},{2,3},{3,0},{4,5},{5,6},{6,7},{7,4},{8,9},{9,10},{10,1... | collective-permute-start | bytes 393224 | tf_op jit(solution)/shard_map/ppermute | solution.py:20
  308.0 48.6 %collective-permute-start.59 = (bf16[256,1024]{1,0:T(8,128)(2,1)}, bf16[256,1024]{1,0:T(8,128)(2,1)S(1)}, u32[]{:S(2)}, u32[]{:S(2)}) collective-permute-start(bf16[256,1024]{1,0:T(8,128)(2,1)} %pad_maximum_fusion.10), channel_id=1, source_target_pairs={{0,3},{1,0},{2,1},{3,2},{4,7},{5,4},{6,5},{7,6},{8,11},{9,8},{10,9... | collective-permute-start | bytes 1572872 | tf_op jit(solution)/shard_map/ppermute | solution.py:20
  309.9 37.4 %collective-permute-start.60 = (bf16[256,1024]{1,0:T(8,128)(2,1)}, bf16[256,1024]{1,0:T(8,128)(2,1)S(1)}, u32[]{:S(2)}, u32[]{:S(2)}) collective-permute-start(bf16[256,1024]{1,0:T(8,128)(2,1)} %pad_maximum_fusion.10), channel_id=1, source_target_pairs={{0,1},{1,2},{2,3},{3,0},{4,5},{5,6},{6,7},{7,4},{8,9},{9,10},{10,1... | collective-permute-start | bytes 1572872 | tf_op jit(solution)/shard_map/ppermute | solution.py:20
  330.3 26.5 %collective-permute-start.52 = (bf16[256,1024]{1,0:T(8,128)(2,1)}, bf16[256,1024]{1,0:T(8,128)(2,1)S(1)}, u32[]{:S(2)}, u32[]{:S(2)}) collective-permute-start(bf16[256,1024]{1,0:T(8,128)(2,1)} %pad_maximum_fusion.9), channel_id=1, source_target_pairs={{0,12},{4,0},{8,4},{12,8},{1,13},{5,1},{9,5},{13,9},{2,14},{6,2},{... | collective-permute-start | bytes 1572872 | tf_op jit(solution)/shard_map/ppermute | solution.py:20
  333.1 23.6 %collective-permute-start.53 = (bf16[256,1024]{1,0:T(8,128)(2,1)}, bf16[256,1024]{1,0:T(8,128)(2,1)S(1)}, u32[]{:S(2)}, u32[]{:S(2)}) collective-permute-start(bf16[256,1024]{1,0:T(8,128)(2,1)} %pad_maximum_fusion.9), channel_id=1, source_target_pairs={{0,4},{4,8},{8,12},{12,0},{1,5},{5,9},{9,13},{13,1},{2,6},{6,10},{... | collective-permute-start | bytes 1572872 | tf_op jit(solution)/shard_map/ppermute | solution.py:20
  334.8 12.5 %collective-permute-start.125 = (bf16[32,1024]{1,0:T(8,128)(2,1)S(1)}, bf16[32,1024]{1,0:T(8,128)(2,1)S(1)}, u32[]{:S(2)}, u32[]{:S(2)}) collective-permute-start(bf16[32,1024]{1,0:T(8,128)(2,1)S(1)} %get-tuple-element.126), channel_id=1, source_target_pairs={{0,4},{4,8},{8,12},{12,0},{1,5},{5,9},{9,13},{13,1},{2,6},{6,10},{... | collective-permute-start | bytes 196616 | tf_op jit(solution)/shard_map/ppermute | solution.py:20
  408.9 33.6 %collective-permute-start.91 = (bf16[64,1024]{1,0:T(8,128)(2,1)}, bf16[64,1024]{1,0:T(8,128)(2,1)}, u32[]{:S(2)}, u32[]{:S(2)}) collective-permute-start(bf16[64,1024]{1,0:T(8,128)(2,1)} %get-tuple-element.129), channel_id=1, source_target_pairs={{0,12},{4,0},{8,4},{12,8},{1,13},{5,1},{9,5},{13,9},{2,14},{6,2},{... | collective-permute-start | bytes 393224 | tf_op jit(solution)/shard_map/ppermute | solution.py:20
  411.1 33.7 %collective-permute-start.92 = (bf16[64,1024]{1,0:T(8,128)(2,1)}, bf16[64,1024]{1,0:T(8,128)(2,1)}, u32[]{:S(2)}, u32[]{:S(2)}) collective-permute-start(bf16[64,1024]{1,0:T(8,128)(2,1)} %get-tuple-element.129), channel_id=1, source_target_pairs={{0,8},{4,12},{8,0},{12,4},{1,9},{5,13},{9,1},{13,5},{2,10},{6,14},... | collective-permute-start | bytes 393224 | tf_op jit(solution)/shard_map/ppermute | solution.py:20
  439.5 11.1 %collective-permute-start.84 = (bf16[64,1024]{1,0:T(8,128)(2,1)S(1)}, bf16[64,1024]{1,0:T(8,128)(2,1)S(1)}, u32[]{:S(2)}, u32[]{:S(2)}) collective-permute-start(bf16[64,1024]{1,0:T(8,128)(2,1)S(1)} %copy-done.41), channel_id=1, source_target_pairs={{0,3},{1,0},{2,1},{3,2},{4,7},{5,4},{6,5},{7,6},{8,11},{9,8},{10,9... | collective-permute-start | bytes 393224 | tf_op jit(solution)/shard_map/ppermute | solution.py:20
  439.5 13.3 %collective-permute-start.85 = (bf16[64,1024]{1,0:T(8,128)(2,1)S(1)}, bf16[64,1024]{1,0:T(8,128)(2,1)S(1)}, u32[]{:S(2)}, u32[]{:S(2)}) collective-permute-start(bf16[64,1024]{1,0:T(8,128)(2,1)S(1)} %copy-done.41), channel_id=1, source_target_pairs={{0,2},{1,3},{2,0},{3,1},{4,6},{5,7},{6,4},{7,5},{8,10},{9,11},{10,... | collective-permute-start | bytes 393224 | tf_op jit(solution)/shard_map/ppermute | solution.py:20
  442.5 11.1 %collective-permute-start.86 = (bf16[64,1024]{1,0:T(8,128)(2,1)S(1)}, bf16[64,1024]{1,0:T(8,128)(2,1)S(1)}, u32[]{:S(2)}, u32[]{:S(2)}) collective-permute-start(bf16[64,1024]{1,0:T(8,128)(2,1)S(1)} %copy-done.41), channel_id=1, source_target_pairs={{0,1},{1,2},{2,3},{3,0},{4,5},{5,6},{6,7},{7,4},{8,9},{9,10},{10,1... | collective-permute-start | bytes 393224 | tf_op jit(solution)/shard_map/ppermute | solution.py:20
  444.8 11.5 %collective-permute-start.108 = (bf16[4,192,128]{2,1,0:T(8,128)(2,1)S(1)}, bf16[4,192,128]{2,1,0:T(8,128)(2,1)S(1)}, u32[]{:S(2)}, u32[]{:S(2)}) collective-permute-start(bf16[4,192,128]{2,1,0:T(8,128)(2,1)S(1)} %get-tuple-element.92), channel_id=1, source_target_pairs={{0,3},{1,0},{2,1},{3,2},{4,7},{5,4},{6,5},{7,6},{8,11},{9,8},{10,9... | collective-permute-start | bytes 589832 | tf_op jit(solution)/shard_map/ppermute | solution.py:20
  445.2 12.7 %collective-permute-start.109 = (bf16[4,192,128]{2,1,0:T(8,128)(2,1)S(1)}, bf16[4,192,128]{2,1,0:T(8,128)(2,1)S(1)}, u32[]{:S(2)}, u32[]{:S(2)}) collective-permute-start(bf16[4,192,128]{2,1,0:T(8,128)(2,1)S(1)} %get-tuple-element.91), channel_id=1, source_target_pairs={{0,2},{1,3},{2,0},{3,1},{4,6},{5,7},{6,4},{7,5},{8,10},{9,11},{10,... | collective-permute-start | bytes 589832 | tf_op jit(solution)/shard_map/ppermute | solution.py:20
  452.8 39.8 %collective-permute-start.94 = (bf16[256,1024]{1,0:T(8,128)(2,1)S(1)}, bf16[256,1024]{1,0:T(8,128)(2,1)S(1)}, u32[]{:S(2)}, u32[]{:S(2)}) collective-permute-start(bf16[256,1024]{1,0:T(8,128)(2,1)S(1)} %pad_maximum_fusion.17), channel_id=1, source_target_pairs={{0,3},{1,0},{2,1},{3,2},{4,7},{5,4},{6,5},{7,6},{8,11},{9,8},{10,9... | collective-permute-start | bytes 1572872 | tf_op jit(solution)/shard_map/ppermute | solution.py:20
  453.6 41.3 %collective-permute-start.95 = (bf16[256,1024]{1,0:T(8,128)(2,1)S(1)}, bf16[256,1024]{1,0:T(8,128)(2,1)S(1)}, u32[]{:S(2)}, u32[]{:S(2)}) collective-permute-start(bf16[256,1024]{1,0:T(8,128)(2,1)S(1)} %pad_maximum_fusion.17), channel_id=1, source_target_pairs={{0,1},{1,2},{2,3},{3,0},{4,5},{5,6},{6,7},{7,4},{8,9},{9,10},{10,1... | collective-permute-start | bytes 1572872 | tf_op jit(solution)/shard_map/ppermute | solution.py:20
  456.4 39.5 %collective-permute-start.87 = (bf16[256,1024]{1,0:T(8,128)(2,1)S(1)}, bf16[256,1024]{1,0:T(8,128)(2,1)S(1)}, u32[]{:S(2)}, u32[]{:S(2)}) collective-permute-start(bf16[256,1024]{1,0:T(8,128)(2,1)S(1)} %pad_maximum_fusion.16), channel_id=1, source_target_pairs={{0,12},{4,0},{8,4},{12,8},{1,13},{5,1},{9,5},{13,9},{2,14},{6,2},{... | collective-permute-start | bytes 1572872 | tf_op jit(solution)/shard_map/ppermute | solution.py:20
  457.8 38.2 %collective-permute-start.88 = (bf16[256,1024]{1,0:T(8,128)(2,1)S(1)}, bf16[256,1024]{1,0:T(8,128)(2,1)S(1)}, u32[]{:S(2)}, u32[]{:S(2)}) collective-permute-start(bf16[256,1024]{1,0:T(8,128)(2,1)S(1)} %pad_maximum_fusion.16), channel_id=1, source_target_pairs={{0,4},{4,8},{8,12},{12,0},{1,5},{5,9},{9,13},{13,1},{2,6},{6,10},{... | collective-permute-start | bytes 1572872 | tf_op jit(solution)/shard_map/ppermute | solution.py:20
  459.5 12.2 %collective-permute-start.111 = (bf16[4,192,128]{2,1,0:T(8,128)(2,1)S(1)}, bf16[4,192,128]{2,1,0:T(8,128)(2,1)S(1)}, u32[]{:S(2)}, u32[]{:S(2)}) collective-permute-start(bf16[4,192,128]{2,1,0:T(8,128)(2,1)S(1)} %get-tuple-element.87), channel_id=1, source_target_pairs={{0,12},{4,0},{8,4},{12,8},{1,13},{5,1},{9,5},{13,9},{2,14},{6,2},{... | collective-permute-start | bytes 589832 | tf_op jit(solution)/shard_map/ppermute | solution.py:20
  492.6 15.0 %collective-permute-start.130 = (bf16[128,1024]{1,0:T(8,128)(2,1)S(1)}, bf16[128,1024]{1,0:T(8,128)(2,1)S(1)}, u32[]{:S(2)}, u32[]{:S(2)}) collective-permute-start(bf16[128,1024]{1,0:T(8,128)(2,1)S(1)} %add_convert_fusion.5), channel_id=1, source_target_pairs={{0,96},{32,0},{64,32},{96,64},{1,97},{33,1},{65,33},{97,65},{2,98}... | collective-permute-start | bytes 786440 | tf_op jit(solution)/shard_map/ppermute | solution.py:20
  494.9 13.5 %collective-permute-start.131 = (bf16[128,1024]{1,0:T(8,128)(2,1)S(1)}, bf16[128,1024]{1,0:T(8,128)(2,1)S(1)}, u32[]{:S(2)}, u32[]{:S(2)}) collective-permute-start(bf16[128,1024]{1,0:T(8,128)(2,1)S(1)} %add_convert_fusion.5), channel_id=1, source_target_pairs={{0,32},{32,64},{64,96},{96,0},{1,33},{33,65},{65,97},{97,1},{2,34}... | collective-permute-start | bytes 786440 | tf_op jit(solution)/shard_map/ppermute | solution.py:20
  495.8 12.9 %collective-permute-start.96 = (bf16[128,1024]{1,0:T(8,128)(2,1)S(1)}, bf16[128,1024]{1,0:T(8,128)(2,1)S(1)}, u32[]{:S(2)}, u32[]{:S(2)}) collective-permute-start(bf16[128,1024]{1,0:T(8,128)(2,1)S(1)} %slice.901), channel_id=1, source_target_pairs={{0,1},{1,2},{2,3},{3,0},{4,5},{5,6},{6,7},{7,4},{8,9},{9,10},{10,1... | collective-permute-start | bytes 786440 | tf_op jit(solution)/shard_map/ppermute | solution.py:20
  496.0 12.7 %collective-permute-start.97 = (bf16[128,1024]{1,0:T(8,128)(2,1)S(1)}, bf16[128,1024]{1,0:T(8,128)(2,1)S(1)}, u32[]{:S(2)}, u32[]{:S(2)}) collective-permute-start(bf16[128,1024]{1,0:T(8,128)(2,1)S(1)} %slice.902), channel_id=1, source_target_pairs={{0,3},{1,0},{2,1},{3,2},{4,7},{5,4},{6,5},{7,6},{8,11},{9,8},{10,9... | collective-permute-start | bytes 786440 | tf_op jit(solution)/shard_map/ppermute | solution.py:20
  508.6 21.1 %collective-permute-start.132 = (bf16[128,1024]{1,0:T(8,128)(2,1)S(1)}, bf16[128,1024]{1,0:T(8,128)(2,1)S(1)}, u32[]{:S(2)}, u32[]{:S(2)}) collective-permute-start(bf16[128,1024]{1,0:T(8,128)(2,1)S(1)} %add_convert_fusion.4), channel_id=1, source_target_pairs={{0,16},{16,0},{1,17},{17,1},{2,18},{18,2},{3,19},{19,3},{4,20},{20... | collective-permute-start | bytes 786440 | tf_op jit(solution)/shard_map/ppermute | solution.py:406
  (163 other events, 1057.3 us)
Sparse Core Ops, SparseCore 0:
  169.2 33.2 reduce-scatter.1
Sparse Core Ops, SparseCore 1:
  174.0 72.6 all-gather.5
  326.7 26.2 all-gather.3
